TPU v7x, 512 devices: a whole 4x4x16 slice. The times are simulated.
512 devices in a mesh: batch: 16 (over y, x), centre: 32 (over z, core).
Axes of the slice: x: 4, y: 4, z: 16, core: 2. Of those that a mesh axis runs over, the one named last changes fastest.
Arguments:
- pool: float32 [4096, 1024], P('batch', 'centre'), may hold values from -4.5 to 4.5
- sample_index: int32 [2048], P('batch'), may hold values from 0 to 255
- targets: float32 [2048, 256], P('batch'), may hold values from -6 to 6
- centres: float32 [8192, 1024], P(('batch', 'centre')), may hold values from -4.5 to 4.5
- coeffs: float32 [8192, 256], P(('batch', 'centre')), may hold values from -6 to 6
- eigvecs: float32 [8192, 1024], P(('batch', 'centre')), may hold values from -0.1875 to 0.1875
- eigscale: float32 [1024], replicated, may hold values from 0.1 to 0.95
Outputs:
- new_coeffs: float32 [8192, 256], P(('batch', 'centre'))
Inputs may be any that keep to these rules, and one draw needn't show every extreme that they name: `sample_index`: each batch row's sample lies in the block of 256 training samples held by its own batch group; the index counts within that block.
All inputs are finite; a program needn't handle non-finite values.
Results may differ from a plain program's by a relative error of at most 0.0003.
Values sent between devices are 32-bit elements; how exact they have to be, the bound alone decides.
No kernel may reach another device: no remote copies, remote signals or barrier semaphores. Data moves between devices by JAX's collectives and lax.ppermute only.
A program may use at most 64 MiB of HBM per device.

v0:
```python
import jax
import jax.numpy as jnp
from jax import lax
from jax.sharding import Mesh
from jax.sharding import PartitionSpec as P

CENTRE = ("centre_0", "centre_1")
BATCH = ("batch_0", "batch_1")
BATCH_CENTRE = ("batch_0", "batch_1", "centre_0", "centre_1")


def joined_along(blocks, dim):
    lengths = list(blocks.shape[1:])
    lengths[dim] *= blocks.shape[0]
    return jnp.moveaxis(blocks, 0, dim).reshape(lengths)


def copy_for_each(value, axis):
    copies = jnp.broadcast_to(value, (lax.axis_size(axis), *value.shape))
    return lax.all_to_all(copies, axis, split_axis=0, concat_axis=0, tiled=True)


def gathered_copies(value, axis, dim):
    return joined_along(copy_for_each(value, axis), dim)


def side_by_side(arrays, axis, dim, along):
    ends, at = ([], 0)
    for a in arrays[:-1]:
        at += a.shape[along]
        ends.append(at)
    both = jnp.concatenate(arrays, axis=along)
    return tuple(jnp.split(lax.all_gather(both, axis, axis=dim, tiled=True), ends, axis=along))


def split_up(value, dim, peers):
    lengths = value.shape
    blocks = value.reshape(*lengths[:dim], peers, lengths[dim] // peers, *lengths[dim + 1 :])
    return jnp.moveaxis(blocks, dim, 0)


def sent_and_summed(value, axis, dim):
    peers = lax.axis_size(axis)
    blocks = lax.all_to_all(split_up(value, dim, peers), axis, 0, 0, tiled=True)
    return jnp.sum(blocks, axis=0)


def filled_up(lines, peers):
    spare = -lines.shape[0] % peers
    if not spare:
        return lines
    return jnp.concatenate([lines, jnp.zeros((spare, *lines.shape[1:]), lines.dtype)])


def sum_by_parts(value, axes):
    lines = value.reshape(-1, value.shape[-1])
    own = sent_and_summed(filled_up(lines, lax.axis_size(axes)), axes, 0)
    whole = gathered_copies(own, axes, 0)
    return whole[: len(lines)].reshape(value.shape)


def summed_rows(value, axes, dim):
    far, near = axes
    blocks = split_up(value, dim, lax.axis_size(far))
    nearer = sent_and_summed(blocks, near, dim + 1)
    arrived = lax.all_to_all(nearer, far, split_axis=0, concat_axis=0, tiled=True)
    return arrived.sum(axis=0)


def gather_axes(value, axes, dim):
    far, near = axes
    initial = copy_for_each(value, far)
    blocks = jnp.swapaxes(copy_for_each(initial, near), 0, 1)
    return joined_along(blocks.reshape(-1, *value.shape), dim)


def total_of(value, axes):
    lines = value.reshape(-1, value.shape[-1])
    own = summed_rows(filled_up(lines, lax.axis_size(axes[0]) * lax.axis_size(axes[1])), axes, 0)
    whole = gather_axes(own, axes, 0)
    return whole[: len(lines)].reshape(value.shape)


def on_device(pool, sample_index, targets, centres, coeffs, eigvecs, eigscale):
    highest = lax.Precision.HIGHEST
    picked = jnp.take(pool, sample_index, axis=0)
    batch_x = gathered_copies(picked, CENTRE, 1)
    row_count = batch_x.shape[0]
    n_batch = lax.axis_size(BATCH)
    n_centre = lax.axis_size(CENTRE)
    own_centres = centres.shape[0]
    group_rows = own_centres * n_batch
    total_centres = group_rows * n_centre
    total_rows = row_count * n_batch
    width = batch_x.shape[1]
    inv_width = 1.0 / jnp.sqrt(jnp.float32(width))
    model_norm = 1.0 / jnp.sqrt(jnp.float32(total_centres))
    zrows, crows = side_by_side((centres, coeffs), BATCH, 0, 1)
    scores = lax.dot_general(
        batch_x,
        zrows,
        (((1,), (1,)), ((), ())),
        precision=highest,
        preferred_element_type=jnp.float32,
    )
    kpiece = jnp.exp(scores * inv_width)
    partial_value = jnp.dot(kpiece, crows, precision=highest, preferred_element_type=jnp.float32)
    kernel, partial_value = (kpiece, partial_value)
    residual = sum_by_parts(partial_value, CENTRE) * model_norm - targets
    gradient = (
        sent_and_summed(
            lax.dot_general(
                kernel,
                residual,
                (((0,), (0,)), ((), ())),
                precision=highest,
                preferred_element_type=jnp.float32,
            ),
            BATCH,
            0,
        )
        * model_norm
    )
    local_coords = lax.dot_general(
        eigvecs,
        gradient,
        (((0,), (0,)), ((), ())),
        precision=highest,
        preferred_element_type=jnp.float32,
    )
    coords = total_of(local_coords, (("batch_0", "batch_1"), ("centre_0", "centre_1")))
    correction = jnp.dot(
        eigvecs, eigscale[:, None] * coords, precision=highest, preferred_element_type=jnp.float32
    )
    step_size = 0.5 * jnp.sqrt(jnp.float32(total_centres) / jnp.float32(total_rows))
    return coeffs - step_size * (gradient - correction)


def solution(mesh):
    finer = Mesh(mesh.devices.reshape(4, 4, 16, 2), ("batch_0", "batch_1", "centre_0", "centre_1"))
    placed = (
        P(BATCH, CENTRE),
        P(BATCH),
        P(BATCH, None),
        P(BATCH_CENTRE, None),
        P(BATCH_CENTRE, None),
        P(BATCH_CENTRE, None),
        P(),
    )
    return jax.shard_map(
        on_device, mesh=finer, in_specs=placed, out_specs=P(BATCH_CENTRE, None), check_vma=False
    )
```

profile of v0, /device:TPU:1, one launch (start us, length us, event | category | flops | bytes accessed | tf_op | source)
XLA Modules:
  0.0 294.5 jit_solution(10606523814920950486)
XLA Ops:
  6.5 1.5 pad_maximum_fusion
  8.1 0.9 copy.26
  8.9 0.7 compare_select_fusion
  9.6 0.6 gather_fusion
  10.3 0.7 compare_and_fusion
  11.1 50.1 %all_to_all.40 = f32[32,128,32]{1,2,0:T(8,128)S(1)} all-to-all(f32[32,128,32]{1,2,0:T(8,128)S(1)} %broadcast_in_dim.28), channel_id=1, replica_groups=mesh['batch_0'=4,'batch_1'=4,'centre_0'=16,'centre_1'=2] {'centre_0','ce..., dimensions={0} | all-to-all | bytes 1048576 | tf_op jit(solution)/shard_map/all_to_all | solution.py:20
  61.2 12.3 %all-gather.2.cloned.1.call-done = f32[256,1280]{1,0:T(8,128)} async-done(((f32[16,1280]{1,0:T(8,128)}), f32[256,1280]{1,0:T(8,128)}) %all-gather.2.cloned.1.call-update) | async-done | bytes 1310736 | tf_op jit(solution)/shard_map/all_gather | solution.py:33
  73.5 2.2 fusion
  75.8 1.3 fusion.6
  77.1 29.5 %all_to_all.41 = f32[32,4,256]{2,1,0:T(4,128)S(1)} all-to-all(f32[32,4,256]{2,1,0:T(4,128)S(1)} %reshape.19), channel_id=1, replica_groups=mesh['batch_0'=4,'batch_1'=4,'centre_0'=16,'centre_1'=2] {'centre_0','ce..., dimensions={0} | all-to-all | bytes 262144 | tf_op jit(solution)/shard_map/all_to_all | solution.py:44
  106.7 20.4 %all_to_all.42 = f32[32,4,256]{2,1,0:T(4,128)S(1)} all-to-all(f32[32,4,256]{2,1,0:T(4,128)S(1)} %broadcast_in_dim.29), channel_id=1, replica_groups=mesh['batch_0'=4,'batch_1'=4,'centre_0'=16,'centre_1'=2] {'centre_0','ce..., dimensions={0} | all-to-all | bytes 262144 | tf_op jit(solution)/shard_map/all_to_all | solution.py:20
  127.2 0.4 fusion.8
  127.6 12.1 %all_to_all.43 = f32[16,16,256]{2,1,0:T(8,128)S(1)} all-to-all(f32[16,16,256]{2,1,0:T(8,128)S(1)} %bitcast.22), channel_id=1, replica_groups=mesh['batch_0'=4,'batch_1'=4,'centre_0'=16,'centre_1'=2] {'batch_0','bat..., dimensions={0} | all-to-all | bytes 524288 | tf_op jit(solution)/shard_map/all_to_all | solution.py:44
  139.7 1.0 convolution_bitcast_fusion
  141.1 0.6 reshape_reshape.6
  141.7 0.6 copy.29
  142.3 61.2 %all_to_all.44 = f32[32,16,2,256]{3,2,1,0:T(2,128)S(1)} all-to-all(f32[32,16,2,256]{3,2,1,0:T(2,128)S(1)} %copy.29), channel_id=1, replica_groups=mesh['batch_0'=4,'batch_1'=4,'centre_0'=16,'centre_1'=2] {'centre_0','ce..., dimensions={0} | all-to-all | bytes 2097152 | tf_op jit(solution)/shard_map/all_to_all | solution.py:44
  203.8 9.1 %all_to_all.45 = f32[16,2,256]{2,1,0:T(2,128)S(1)} all-to-all(f32[16,2,256]{2,1,0:T(2,128)S(1)} %reduce_sum.38), channel_id=1, replica_groups=mesh['batch_0'=4,'batch_1'=4,'centre_0'=16,'centre_1'=2] {'batch_0','bat..., dimensions={0} | all-to-all | bytes 65536 | tf_op jit(solution)/shard_map/all_to_all | solution.py:66
  212.9 9.5 %all_to_all.46 = f32[16,2,256]{2,1,0:T(2,128)S(1)} all-to-all(f32[16,2,256]{2,1,0:T(2,128)S(1)} %broadcast_in_dim.30), channel_id=1, replica_groups=mesh['batch_0'=4,'batch_1'=4,'centre_0'=16,'centre_1'=2] {'batch_0','bat..., dimensions={0} | all-to-all | bytes 65536 | tf_op jit(solution)/shard_map/all_to_all | solution.py:20
  222.4 0.5 broadcast_in_dim.31
  222.9 62.2 %all_to_all.47 = f32[32,16,2,256]{3,2,1,0:T(2,128)S(1)} all-to-all(f32[32,16,2,256]{3,2,1,0:T(2,128)S(1)} %broadcast_in_dim.31), channel_id=1, replica_groups=mesh['batch_0'=4,'batch_1'=4,'centre_0'=16,'centre_1'=2] {'centre_0','ce..., dimensions={0} | all-to-all | bytes 2097152 | tf_op jit(solution)/shard_map/all_to_all | solution.py:20
  285.0 0.5 copy.31
  285.6 0.7 reshape_reshape.7
  286.3 1.3 fusion.2
  (24 shorter events, 1.2 us)
Async XLA Ops:
  6.5 133.2 %copy-start = (f32[16,1024]{1,0:T(8,128)S(1)}, f32[16,1024]{1,0:T(8,128)}, u32[]{:S(2)}) copy-start(f32[16,1024]{1,0:T(8,128)} %param.12) | copy-start | bytes 196612
  6.5 67.0 %all-gather.2.cloned.1.call-start = ((), (), s32[]{:S(2)}) async-start(), calls=%async_computation.8 | async-start | bytes 1392640 | tf_op jit(solution)/shard_map/all_gather | solution.py:33
  75.8 51.4 %copy-start.1 = (f32[128,256]{1,0:T(8,128)S(1)}, f32[128,256]{1,0:T(8,128)}, u32[]{:S(2)}) copy-start(f32[128,256]{1,0:T(8,128)} %param.9) | copy-start | bytes 393220
  285.6 0.8 copy-start.2
  285.6 0.8 copy-start.3
Sparse Core Ops, SparseCore 0:
  10.4 63.1 all-gather.1
where the time goes:
time: 295 us
  blocking collectives  254 us (86%)
  between operations  13.6 us (5%)
  waiting for transfers between devices  12.3 us (4%)
  matrix products  6.26 us (2%)
  local copies, waits for them, and re-layouts  5.01 us (2%)
  other arithmetic  3.4 us (1%)
    all_to_all x4, blocking collectives, copy_for_each(): return lax.all_to_all(copies, axis, split_axis=0, concat_axis=0, tiled=True)  142 us
    all_to_all x3, blocking collectives, sent_and_summed(): blocks = lax.all_to_all(split_up(value, dim, peers), axis, 0, 0, tiled=True)  103 us
    all_gather x1, waiting for transfers between devices, side_by_side(): lax.all_gather(both, axis, axis=dim, tiled=True)  12.3 us
    all_to_all x1, blocking collectives, summed_rows(): lax.all_to_all(nearer, far, split_axis=0, concat_axis=0, tiled=True)  9.07 us
  transfers between devices with their start and end apart: 1, of which 1 were waited for; matrix products, arithmetic and copies ran while one was open for 1% of the time, Pallas kernels for 0%

commit v1 on v0

v1 whole, which is shorter than its diff:
```python
import jax
import jax.numpy as jnp
from jax import lax
from jax.sharding import Mesh
from jax.sharding import PartitionSpec as P

PLANE = ("y", "x")
LINE = "z"
CORE = "core"
EVERY = ("y", "x", "z", "core")
HIGHEST = lax.Precision.HIGHEST


def product(left, right, left_dim, right_dim):
    return lax.dot_general(
        left,
        right,
        (((left_dim,), (right_dim,)), ((), ())),
        precision=HIGHEST,
        preferred_element_type=jnp.float32,
    )


def swapped(value):
    return lax.ppermute(value, CORE, [(0, 1), (1, 0)])


def exchanged(blocks, axis):
    return lax.all_to_all(blocks, axis, split_axis=0, concat_axis=0, tiled=True)


def to_all(value, axis):
    return exchanged(jnp.broadcast_to(value, (lax.axis_size(axis), *value.shape)), axis)


def on_device(pool, sample_index, targets, centres, coeffs, eigvecs, eigscale):
    n_plane = lax.axis_size(PLANE)
    n_line = lax.axis_size(LINE)
    n_core = lax.axis_size(CORE)
    own = centres.shape[0]
    rows = sample_index.shape[0]
    half = rows // n_core
    feats = pool.shape[1]
    width = centres.shape[1]
    outs = coeffs.shape[1]
    total_centres = own * n_plane * n_line * n_core
    total_rows = rows * n_plane
    core = lax.axis_index(CORE)

    merged = jnp.concatenate([centres, coeffs, eigvecs], axis=1)
    mine = to_all(merged, PLANE).reshape(own * n_plane, -1)
    other = swapped(mine)

    picked = jnp.take(pool, sample_index, axis=0).reshape(n_core, half, feats)
    keep = lax.dynamic_index_in_dim(picked, core, 0, keepdims=False)
    give = lax.dynamic_index_in_dim(picked, 1 - core, 0, keepdims=False)
    come = swapped(give)
    pair = jnp.where(core == 0, jnp.stack([keep, come]), jnp.stack([come, keep]))
    pair = pair.transpose(0, 2, 1).reshape(n_core * feats // 2, 2 * half)
    batch_t = to_all(pair, LINE).reshape(width, half)

    def kernel_of(z):
        return jnp.exp(product(batch_t, z, 0, 1) * (1.0 / jnp.sqrt(jnp.float32(width))))

    k_mine = kernel_of(mine[:, :width])
    k_other = kernel_of(other[:, :width])
    part = product(k_mine, mine[:, width:], 1, 0) + product(k_other, other[:, width:], 1, 0)
    part = exchanged(part.reshape(n_line, half // n_line, -1), LINE).sum(axis=0)
    whole = to_all(part, LINE).reshape(half, -1)

    model_norm = 1.0 / jnp.sqrt(jnp.float32(total_centres))
    own_targets = lax.dynamic_slice_in_dim(targets, core * half, half, 0)
    residual = whole[:, :outs] * model_norm - own_targets
    scaled = whole[:, outs:] * eigscale

    def change_of(k, v):
        return product(k - product(scaled, v, 1, 1), residual, 0, 0)

    change = change_of(k_mine, mine[:, width + outs :]) + swapped(
        change_of(k_other, other[:, width + outs :])
    )
    change = exchanged(change.reshape(n_plane, own, outs), PLANE).sum(axis=0)
    step_size = 0.5 * jnp.sqrt(jnp.float32(total_centres) / jnp.float32(total_rows))
    return coeffs - (step_size * model_norm) * change


def solution(mesh):
    finer = Mesh(mesh.devices.reshape(4, 4, 16, 2), EVERY)
    placed = (
        P(PLANE, (LINE, CORE)),
        P(PLANE),
        P(PLANE, None),
        P(EVERY, None),
        P(EVERY, None),
        P(EVERY, None),
        P(),
    )
    return jax.shard_map(
        on_device, mesh=finer, in_specs=placed, out_specs=P(EVERY, None), check_vma=False
    )
```

time: 295 us -> 160 us (0.54)
  blocking collectives: 254 us -> 101 us
  starting transfers between devices: 0.01 us -> 27.1 us
  between operations: 13.6 us -> 0.23 us
  matrix products: 6.26 us -> 10.6 us
  waiting for transfers between devices: 12.3 us -> 16.4 us
    all_to_all x8 -> x4, blocking collectives: 254 us -> 101 us  [exchanged(): return lax.all_to_all(blocks, axis, split_axis=0, concat_axis=0, tiled=True)]
    ppermute x0 -> x3, starting transfers between devices: none -> 15.5 us  [swapped(): return lax.ppermute(value, CORE, [(0, 1), (1, 0)])]
    all_to_all x0 -> x1, waiting for transfers between devices: none -> 15.1 us  [exchanged(): return lax.all_to_all(blocks, axis, split_axis=0, concat_axis=0, tiled=True)]
    all_gather x1 -> x0, waiting for transfers between devices: 12.3 us -> none  [side_by_side(): lax.all_gather(both, axis, axis=dim, tiled=True)]
    all_to_all x0 -> x1, starting transfers between devices: none -> 11.6 us  [exchanged(): return lax.all_to_all(blocks, axis, split_axis=0, concat_axis=0, tiled=True)]
    dot_general x5 -> x8, matrix products: 6.26 us -> 10.6 us  [product(): lax.dot_general(left, right, (((left_dim,), (right_dim,)), ((), ())), pre...]
  transfers between devices with their start and end apart: 1 -> 4, of which waited for: 1 -> 3; matrix products, arithmetic and copies ran while one was open for 1% -> 3% of each run, Pallas kernels for 0% -> 0%
where the time goes in v1:
time: 160 us; the launch traced here: 159 us
  blocking collectives  101 us (63%)
  starting transfers between devices  27.1 us (17%)
  waiting for transfers between devices  16.4 us (10%)
  matrix products  10.6 us (7%)
  local copies, waits for them, and re-layouts  2.37 us (1%)
  other arithmetic  1.63 us (1%)
    all_to_all x4, blocking collectives, exchanged(): return lax.all_to_all(blocks, axis, split_axis=0, concat_axis=0, tiled=True)  101 us
    ppermute x3, starting transfers between devices, swapped(): return lax.ppermute(value, CORE, [(0, 1), (1, 0)])  15.5 us
    all_to_all x1, waiting for transfers between devices, exchanged(): return lax.all_to_all(blocks, axis, split_axis=0, concat_axis=0, tiled=True)  15.1 us
    all_to_all x1, starting transfers between devices, exchanged(): return lax.all_to_all(blocks, axis, split_axis=0, concat_axis=0, tiled=True)  11.6 us
    dot_general x8, matrix products, product(): lax.dot_general(left, right, (((left_dim,), (right_dim,)), ((), ())), pre...  10.6 us
  transfers between devices with their start and end apart: 4, of which 3 were waited for; matrix products, arithmetic and copies ran while one was open for 3% of the time, Pallas kernels for 0%

profile of v1, /device:TPU:1, one launch (start us, length us, event | category | flops | bytes accessed | tf_op | source)
XLA Modules:
  0.0 159.2 jit_solution(4286217605706608892)
XLA Ops:
  0.0 0.9 pad_maximum_fusion
  0.9 0.2 broadcast_in_dim.29
  1.2 37.0 %all_to_all.25 = f32[16,16,2304]{2,1,0:T(8,128)S(1)} all-to-all(f32[16,16,2304]{2,1,0:T(8,128)S(1)} %broadcast_in_dim.29), channel_id=1, replica_groups=mesh['y'=4,'x'=4,'z'=16,'core'=2] {'y','x'}, dimensions={0} | all-to-all | bytes 4718592 | tf_op jit(solution)/shard_map/all_to_all | solution.py:29
  38.2 5.2 %collective-permute-start.1 = (f32[256,2304]{1,0:T(8,128)S(1)}, f32[256,2304]{1,0:T(8,128)}, u32[]{:S(2)}, u32[]{:S(2)}) collective-permute-start(f32[256,2304]{1,0:T(8,128)S(1)} %bitcast.14), channel_id=1, source_target_pairs={{0,1},{1,0},{2,3},{3,2},{4,5},{5,4},{6,7},{7,6},{8,9},{9,8},{10,11... | collective-permute-start | bytes 7077896 | tf_op jit(solution)/shard_map/ppermute | solution.py:25
  43.5 0.6 gather_fusion
  44.4 1.9 %collective-permute-start = (f32[64,32]{0,1:T(8,128)S(1)}, f32[64,32]{0,1:T(8,128)S(1)}, u32[]{:S(2)}, u32[]{:S(2)}) collective-permute-start(f32[64,32]{0,1:T(8,128)S(1)} %get-tuple-element.6), channel_id=1, source_target_pairs={{0,1},{1,0},{2,3},{3,2},{4,5},{5,4},{6,7},{7,6},{8,9},{9,8},{10,11... | collective-permute-start | bytes 24584 | tf_op jit(solution)/shard_map/ppermute | solution.py:25
  46.3 1.3 collective-permute-done
  47.7 27.9 %all_to_all.26 = f32[16,32,128]{2,1,0:T(8,128)S(1)} all-to-all(f32[16,32,128]{2,1,0:T(8,128)S(1)} %broadcast_in_dim.28), channel_id=1, replica_groups=mesh['y'=4,'x'=4,'z'=16,'core'=2] {'z'}, dimensions={0} | all-to-all | bytes 524288 | tf_op jit(solution)/shard_map/all_to_all | solution.py:29
  75.6 0.1 reshape.32
  75.8 1.0 fusion.4
  76.8 0.9 fusion.1
  77.7 2.2 %fusion.3 = f32[64,256]{1,0:T(8,128)S(1)} fusion(f32[1024,64]{1,0:T(8,128)S(1)} %reshape.32, f32[256,2304]{1,0:T(8,128)} %collective-permute-done.1), kind=kOutput, calls=%fused_computation.7 | convolution fusion | flops 201342976 | bytes 1376256 | tf_op jit(solution)/shard_map/dot_general | solution.py:15
  79.9 2.2 %convolution_add_fusion = f32[64,1280]{1,0:T(8,128)S(1)} fusion(f32[64,1280]{1,0:T(8,128)S(1)} %fusion.1, f32[64,256]{1,0:T(8,128)S(1)} %fusion.3, f32[256,2304]{1,0:T(8,128)} %collective-permute-done.1), kind=kOutput, calls=%fused_computation.1 | convolution fusion | flops 251740160 | bytes 2031616 | tf_op jit(solution)/shard_map/dot_general | solution.py:15
  82.3 25.3 %all_to_all.27 = f32[16,4,1280]{2,1,0:T(4,128)S(1)} all-to-all(f32[16,4,1280]{2,1,0:T(4,128)S(1)} %reshape.34), channel_id=1, replica_groups=mesh['y'=4,'x'=4,'z'=16,'core'=2] {'z'}, dimensions={0} | all-to-all | bytes 655360 | tf_op jit(solution)/shard_map/all_to_all | solution.py:29
  107.6 0.8 broadcast_in_dim.30
  108.3 11.6 %all-to-all-start.3 = ((f32[16,4,1280]{2,1,0:T(4,128)}), f32[16,4,1280]{2,1,0:T(4,128)S(1)}, u32[]{:S(2)}, u32[]{:S(2)}) async-start(f32[16,4,1280]{2,1,0:T(4,128)} %broadcast_in_dim.30), calls=%async_computation.3 | async-start | bytes 655360 | tf_op jit(solution)/shard_map/all_to_all | solution.py:29
  119.9 15.1 %all-to-all-done.3 = f32[16,4,1280]{2,1,0:T(4,128)S(1)} async-done(((f32[16,4,1280]{2,1,0:T(4,128)}), f32[16,4,1280]{2,1,0:T(4,128)S(1)}, u32[]{:S(2)}, u32[]{:S(2)}) %all-to-all-start.3) | async-done | bytes 327712 | tf_op jit(solution)/shard_map/all_to_all | solution.py:29
  135.1 2.3 %convolution_subtract_fusion = f32[64,256]{1,0:T(8,128)S(1)} fusion(f32[64,256]{1,0:T(8,128)S(1)} %fusion.3, f32[256,2304]{1,0:T(8,128)} %collective-permute-done.1, f32[64,1280]{1,0:T(8,128)S(1)} %reshape.35, f32[1024]{0:T(1024)S(1)} %copy-done.3), kind=kOutput, calls=%fused_computation.10 | convolution fusion | flops 201408512 | bytes 1445888 | tf_op jit(solution)/shard_map/dot_general | solution.py:15
  137.4 0.4 fusion.13
  137.9 8.4 %collective-permute-start.2 = (f32[256,256]{1,0:T(8,128)S(1)}, f32[256,256]{1,0:T(8,128)S(1)}, u32[]{:S(2)}, u32[]{:S(2)}) collective-permute-start(f32[256,256]{1,0:T(8,128)S(1)} %fusion.13), channel_id=1, source_target_pairs={{0,1},{1,0},{2,3},{3,2},{4,5},{5,4},{6,7},{7,6},{8,9},{9,8},{10,11... | collective-permute-start | bytes 786440 | tf_op jit(solution)/shard_map/ppermute | solution.py:25
  146.3 1.1 convolution_subtract_fusion.1
  147.4 0.4 convolution_add_fusion.1
  147.8 10.7 %all_to_all.28 = f32[16,16,256]{2,1,0:T(8,128)S(1)} all-to-all(f32[16,16,256]{2,1,0:T(8,128)S(1)} %bitcast.18), channel_id=1, replica_groups=mesh['y'=4,'x'=4,'z'=16,'core'=2] {'y','x'}, dimensions={0} | all-to-all | bytes 524288 | tf_op jit(solution)/shard_map/all_to_all | solution.py:29
  158.6 0.6 multiply_subtract_fusion
  (27 shorter events, 0.8 us)
Async XLA Ops:
  1.1 42.3 %copy-start.4 = (s32[128]{0:T(128)S(1)}, s32[128]{0:T(128)}, u32[]{:S(2)}) copy-start(s32[128]{0:T(128)} %param.8) | copy-start | bytes 1540
  1.1 42.3 %copy-start.2 = (f32[256,32]{0,1:T(8,128)S(1)}, f32[256,32]{0,1:T(8,128)}, u32[]{:S(2)}) copy-start(f32[256,32]{0,1:T(8,128)} %param.7) | copy-start | bytes 98308
  38.2 39.5 %collective-permute-start.1 = (f32[256,2304]{1,0:T(8,128)S(1)}, f32[256,2304]{1,0:T(8,128)}, u32[]{:S(2)}, u32[]{:S(2)}) collective-permute-start(f32[256,2304]{1,0:T(8,128)S(1)} %bitcast.14), channel_id=1, source_target_pairs={{0,1},{1,0},{2,3},{3,2},{4,5},{5,4},{6,7},{7,6},{8,9},{9,8},{10,11... | collective-permute-start | bytes 7077896 | tf_op jit(solution)/shard_map/ppermute | solution.py:25
  44.4 3.2 %collective-permute-start = (f32[64,32]{0,1:T(8,128)S(1)}, f32[64,32]{0,1:T(8,128)S(1)}, u32[]{:S(2)}, u32[]{:S(2)}) collective-permute-start(f32[64,32]{0,1:T(8,128)S(1)} %get-tuple-element.6), channel_id=1, source_target_pairs={{0,1},{1,0},{2,3},{3,2},{4,5},{5,4},{6,7},{7,6},{8,9},{9,8},{10,11... | collective-permute-start | bytes 24584 | tf_op jit(solution)/shard_map/ppermute | solution.py:25
  79.9 55.2 %copy-start.3 = (f32[1024]{0:T(1024)S(1)}, f32[1024]{0:T(1024)}, u32[]{:S(2)}) copy-start(f32[1024]{0:T(1024)} %param.13) | copy-start | bytes 12292
  82.2 55.3 %copy-start = (f32[128,256]{1,0:T(8,128)S(1)}, f32[128,256]{1,0:T(8,128)}, u32[]{:S(2)}) copy-start(f32[128,256]{1,0:T(8,128)} %param.9) | copy-start | bytes 393220
  108.3 26.6 %all-to-all-start.3 = ((f32[16,4,1280]{2,1,0:T(4,128)}), f32[16,4,1280]{2,1,0:T(4,128)S(1)}, u32[]{:S(2)}, u32[]{:S(2)}) async-start(f32[16,4,1280]{2,1,0:T(4,128)} %broadcast_in_dim.30), calls=%async_computation.3 | async-start | bytes 655360 | tf_op jit(solution)/shard_map/all_to_all | solution.py:29
  135.1 23.5 %copy-start.1 = (f32[16,256]{1,0:T(8,128)S(1)}, f32[16,256]{1,0:T(8,128)}, u32[]{:S(2)}) copy-start(f32[16,256]{1,0:T(8,128)} %param.11) | copy-start | bytes 49156
  137.9 9.5 %collective-permute-start.2 = (f32[256,256]{1,0:T(8,128)S(1)}, f32[256,256]{1,0:T(8,128)S(1)}, u32[]{:S(2)}, u32[]{:S(2)}) collective-permute-start(f32[256,256]{1,0:T(8,128)S(1)} %fusion.13), channel_id=1, source_target_pairs={{0,1},{1,0},{2,3},{3,2},{4,5},{5,4},{6,7},{7,6},{8,9},{9,8},{10,11... | collective-permute-start | bytes 786440 | tf_op jit(solution)/shard_map/ppermute | solution.py:25

commit v2 on v1

--- a/solution.py
+++ b/solution.py
@@ -49,7 +49,6 @@
 
     merged = jnp.concatenate([centres, coeffs, eigvecs], axis=1)
     mine = to_all(merged, PLANE).reshape(own * n_plane, -1)
-    other = swapped(mine)
 
     picked = jnp.take(pool, sample_index, axis=0).reshape(n_core, half, feats)
     keep = lax.dynamic_index_in_dim(picked, core, 0, keepdims=False)
@@ -57,7 +56,10 @@
     come = swapped(give)
     pair = jnp.where(core == 0, jnp.stack([keep, come]), jnp.stack([come, keep]))
     pair = pair.transpose(0, 2, 1).reshape(n_core * feats // 2, 2 * half)
-    batch_t = to_all(pair, LINE).reshape(width, half)
+    batch_t = lax.all_gather(pair, LINE).reshape(width, half)
+
+    mine, batch_t = lax.optimization_barrier((mine, batch_t))
+    other = swapped(mine)
 
     def kernel_of(z):
         return jnp.exp(product(batch_t, z, 0, 1) * (1.0 / jnp.sqrt(jnp.float32(width))))

time: 160 us -> 139 us (0.87)
  blocking collectives: 101 us -> 65.8 us
  starting transfers between devices: 27.1 us -> 40.4 us
  matrix products: 10.6 us -> 8.04 us
  waiting for transfers between devices: 16.4 us -> 18.3 us
  local copies, waits for them, and re-layouts: 2.37 us -> 4.16 us
    all_to_all x4 -> x2, blocking collectives: 101 us -> 36.5 us  [exchanged(): return lax.all_to_all(blocks, axis, split_axis=0, concat_axis=0, tiled=True)]
    all_gather x0 -> x1, blocking collectives: none -> 29.3 us  [on_device(): batch_t = lax.all_gather(pair, LINE).reshape(width, half)]
    all_to_all x1 -> x2, starting transfers between devices: 11.6 us -> 19.3 us  [exchanged(): return lax.all_to_all(blocks, axis, split_axis=0, concat_axis=0, tiled=True)]
    ppermute x3, starting transfers between devices: 15.5 us -> 21.1 us  [swapped(): return lax.ppermute(value, CORE, [(0, 1), (1, 0)])]
    dot_general x8, matrix products: 10.6 us -> 8.04 us  [product(): lax.dot_general(left, right, (((left_dim,), (right_dim,)), ((), ())), pre...]
    ppermute x3, waiting for transfers between devices: 1.31 us -> 3.09 us  [swapped(): return lax.ppermute(value, CORE, [(0, 1), (1, 0)])]
    all_to_all x1 -> x2, waiting for transfers between devices: 15.1 us -> 15.3 us  [exchanged(): return lax.all_to_all(blocks, axis, split_axis=0, concat_axis=0, tiled=True)]
  transfers between devices with their start and end apart: 4 -> 5, of which waited for: 3 -> 4; matrix products, arithmetic and copies ran while one was open for 3% -> 3% of each run, Pallas kernels for 0% -> 0%
where the time goes in v2:
time: 139 us
  blocking collectives  65.8 us (47%)
  starting transfers between devices  40.4 us (29%)
  waiting for transfers between devices  18.3 us (13%)
  matrix products  8.04 us (6%)
  local copies, waits for them, and re-layouts  4.16 us (3%)
  other arithmetic  1.63 us (1%)
    all_to_all x2, blocking collectives, exchanged(): return lax.all_to_all(blocks, axis, split_axis=0, concat_axis=0, tiled=True)  36.5 us
    all_gather x1, blocking collectives, on_device(): batch_t = lax.all_gather(pair, LINE).reshape(width, half)  29.3 us
    ppermute x3, starting transfers between devices, swapped(): return lax.ppermute(value, CORE, [(0, 1), (1, 0)])  21.1 us
    all_to_all x2, starting transfers between devices, exchanged(): return lax.all_to_all(blocks, axis, split_axis=0, concat_axis=0, tiled=True)  19.3 us
    all_to_all x2, waiting for transfers between devices, exchanged(): return lax.all_to_all(blocks, axis, split_axis=0, concat_axis=0, tiled=True)  15.3 us
    dot_general x8, matrix products, product(): lax.dot_general(left, right, (((left_dim,), (right_dim,)), ((), ())), pre...  8.04 us
    ppermute x3, waiting for transfers between devices, swapped(): return lax.ppermute(value, CORE, [(0, 1), (1, 0)])  3.09 us
  transfers between devices with their start and end apart: 5, of which 4 were waited for; matrix products, arithmetic and copies ran while one was open for 3% of the time, Pallas kernels for 0%

profile of v2, /device:TPU:1, one launch (start us, length us, event | category | flops | bytes accessed | tf_op | source)
XLA Modules:
  0.0 138.5 jit_solution(10497046417796825660)
XLA Ops:
  0.0 0.9 pad_maximum_fusion
  0.9 1.6 %broadcast_in_dim.21 = f32[16,16,2304]{2,1,0:T(8,128)} broadcast(f32[16,2304]{1,0:T(8,128)S(1)} %pad_maximum_fusion), dimensions={1,2} | broadcast | bytes 2506752 | tf_op jit(solution)/shard_map/broadcast_in_dim | solution.py:33
  2.6 7.7 %all-to-all-start = ((f32[16,16,2304]{2,1,0:T(8,128)}), f32[16,16,2304]{2,1,0:T(8,128)S(1)}, u32[]{:S(2)}, u32[]{:S(2)}) async-start(f32[16,16,2304]{2,1,0:T(8,128)} %broadcast_in_dim.21), calls=%async_computation | async-start | bytes 4718592 | tf_op jit(solution)/shard_map/all_to_all | solution.py:29
  10.4 0.6 gather_fusion
  11.3 4.9 %collective-permute-start = (f32[64,32]{0,1:T(8,128)S(1)}, f32[64,32]{0,1:T(8,128)S(1)}, u32[]{:S(2)}, u32[]{:S(2)}) collective-permute-start(f32[64,32]{0,1:T(8,128)S(1)} %get-tuple-element.10), channel_id=1, source_target_pairs={{0,1},{1,0},{2,3},{3,2},{4,5},{5,4},{6,7},{7,6},{8,9},{9,8},{10,11... | collective-permute-start | bytes 24584 | tf_op jit(solution)/shard_map/ppermute | solution.py:25
  16.2 0.8 collective-permute-done
  17.1 29.3 %all_gather.3 = f32[16,32,128]{2,1,0:T(8,128)S(1)} all-gather(f32[1,32,128]{2,1,0:T(8,128)S(1)} %all_gather_reshape.3), channel_id=1, replica_groups=mesh['y'=4,'x'=4,'z'=16,'core'=2] {'z'}, dimensions={0}, use_global_device_ids=true | all-gather | bytes 278528 | tf_op jit(solution)/shard_map/all_gather | solution.py:59
  46.5 7.7 %collective-permute-start.1 = (f32[256,2304]{1,0:T(8,128)S(1)}, f32[256,2304]{1,0:T(8,128)S(1)}, u32[]{:S(2)}, u32[]{:S(2)}) collective-permute-start(f32[256,2304]{1,0:T(8,128)S(1)} %bitcast.14), channel_id=1, source_target_pairs={{0,1},{1,0},{2,3},{3,2},{4,5},{5,4},{6,7},{7,6},{8,9},{9,8},{10,11... | collective-permute-start | bytes 7077896 | tf_op jit(solution)/shard_map/ppermute | solution.py:25
  54.2 1.0 fusion.4
  55.3 0.9 fusion.1
  56.1 2.2 %collective-permute-done.1 = f32[256,2304]{1,0:T(8,128)S(1)} collective-permute-done((f32[256,2304]{1,0:T(8,128)S(1)}, f32[256,2304]{1,0:T(8,128)S(1)}, u32[]{:S(2)}, u32[]{:S(2)}) %collective-permute-start.1) | collective-permute-done | bytes 2359328 | tf_op jit(solution)/shard_map/ppermute | solution.py:25
  58.4 1.0 fusion.3
  59.8 0.9 convolution_add_fusion
  60.8 24.6 %all_to_all.20 = f32[16,4,1280]{2,1,0:T(4,128)S(1)} all-to-all(f32[16,4,1280]{2,1,0:T(4,128)S(1)} %reshape.30), channel_id=1, replica_groups=mesh['y'=4,'x'=4,'z'=16,'core'=2] {'z'}, dimensions={0} | all-to-all | bytes 655360 | tf_op jit(solution)/shard_map/all_to_all | solution.py:29
  85.4 0.8 broadcast_in_dim.26
  86.2 11.6 %all-to-all-start.2 = ((f32[16,4,1280]{2,1,0:T(4,128)}), f32[16,4,1280]{2,1,0:T(4,128)S(1)}, u32[]{:S(2)}, u32[]{:S(2)}) async-start(f32[16,4,1280]{2,1,0:T(4,128)} %broadcast_in_dim.26), calls=%async_computation.2 | async-start | bytes 655360 | tf_op jit(solution)/shard_map/all_to_all | solution.py:29
  97.8 15.2 %all-to-all-done.2 = f32[16,4,1280]{2,1,0:T(4,128)S(1)} async-done(((f32[16,4,1280]{2,1,0:T(4,128)}), f32[16,4,1280]{2,1,0:T(4,128)S(1)}, u32[]{:S(2)}, u32[]{:S(2)}) %all-to-all-start.2) | async-done | bytes 327712 | tf_op jit(solution)/shard_map/all_to_all | solution.py:29
  113.2 2.3 %convolution_subtract_fusion = f32[64,256]{1,0:T(8,128)S(1)} fusion(f32[64,256]{1,0:T(8,128)S(1)} %fusion.3, f32[256,2304]{1,0:T(8,128)} %copy-done, f32[64,1280]{1,0:T(8,128)S(1)} %reshape.31, f32[1024]{0:T(1024)S(1)} %copy-done.4), kind=kOutput, calls=%fused_computation.10 | convolution fusion | flops 201408512 | bytes 1445888 | tf_op jit(solution)/shard_map/dot_general | solution.py:15
  115.5 0.4 fusion.13
  115.9 8.5 %collective-permute-start.2 = (f32[256,256]{1,0:T(8,128)S(1)}, f32[256,256]{1,0:T(8,128)S(1)}, u32[]{:S(2)}, u32[]{:S(2)}) collective-permute-start(f32[256,256]{1,0:T(8,128)S(1)} %fusion.13), channel_id=1, source_target_pairs={{0,1},{1,0},{2,3},{3,2},{4,5},{5,4},{6,7},{7,6},{8,9},{9,8},{10,11... | collective-permute-start | bytes 786440 | tf_op jit(solution)/shard_map/ppermute | solution.py:25
  124.4 1.1 convolution_subtract_fusion.1
  125.5 0.4 convolution_add_fusion.1
  125.9 11.9 %all_to_all.21 = f32[16,16,256]{2,1,0:T(8,128)S(1)} all-to-all(f32[16,16,256]{2,1,0:T(8,128)S(1)} %bitcast.18), channel_id=1, replica_groups=mesh['y'=4,'x'=4,'z'=16,'core'=2] {'y','x'}, dimensions={0} | all-to-all | bytes 524288 | tf_op jit(solution)/shard_map/all_to_all | solution.py:29
  137.9 0.6 multiply_subtract_fusion
  (29 shorter events, 1.3 us)
Async XLA Ops:
  2.5 7.7 %copy-start.3 = (f32[256,32]{0,1:T(8,128)S(1)}, f32[256,32]{0,1:T(8,128)}, u32[]{:S(2)}) copy-start(f32[256,32]{0,1:T(8,128)} %param.7) | copy-start | bytes 98308
  2.6 7.8 %copy-start.5 = (s32[128]{0:T(128)S(1)}, s32[128]{0:T(128)}, u32[]{:S(2)}) copy-start(s32[128]{0:T(128)} %param.8) | copy-start | bytes 1540
  2.6 44.0 %all-to-all-start = ((f32[16,16,2304]{2,1,0:T(8,128)}), f32[16,16,2304]{2,1,0:T(8,128)S(1)}, u32[]{:S(2)}, u32[]{:S(2)}) async-start(f32[16,16,2304]{2,1,0:T(8,128)} %broadcast_in_dim.21), calls=%async_computation | async-start | bytes 4718592 | tf_op jit(solution)/shard_map/all_to_all | solution.py:29
  11.3 5.7 %collective-permute-start = (f32[64,32]{0,1:T(8,128)S(1)}, f32[64,32]{0,1:T(8,128)S(1)}, u32[]{:S(2)}, u32[]{:S(2)}) collective-permute-start(f32[64,32]{0,1:T(8,128)S(1)} %get-tuple-element.10), channel_id=1, source_target_pairs={{0,1},{1,0},{2,3},{3,2},{4,5},{5,4},{6,7},{7,6},{8,9},{9,8},{10,11... | collective-permute-start | bytes 24584 | tf_op jit(solution)/shard_map/ppermute | solution.py:25
  46.5 11.8 %collective-permute-start.1 = (f32[256,2304]{1,0:T(8,128)S(1)}, f32[256,2304]{1,0:T(8,128)S(1)}, u32[]{:S(2)}, u32[]{:S(2)}) collective-permute-start(f32[256,2304]{1,0:T(8,128)S(1)} %bitcast.14), channel_id=1, source_target_pairs={{0,1},{1,0},{2,3},{3,2},{4,5},{5,4},{6,7},{7,6},{8,9},{9,8},{10,11... | collective-permute-start | bytes 7077896 | tf_op jit(solution)/shard_map/ppermute | solution.py:25
  58.4 1.4 %copy-start = (f32[256,2304]{1,0:T(8,128)}, f32[256,2304]{1,0:T(8,128)S(1)}, u32[]{:S(2)}) copy-start(f32[256,2304]{1,0:T(8,128)S(1)} %collective-permute-done.1) | copy-start | bytes 7077892
  59.8 53.3 %copy-start.4 = (f32[1024]{0:T(1024)S(1)}, f32[1024]{0:T(1024)}, u32[]{:S(2)}) copy-start(f32[1024]{0:T(1024)} %param.13) | copy-start | bytes 12292
  60.7 54.8 %copy-start.1 = (f32[128,256]{1,0:T(8,128)S(1)}, f32[128,256]{1,0:T(8,128)}, u32[]{:S(2)}) copy-start(f32[128,256]{1,0:T(8,128)} %param.9) | copy-start | bytes 393220
  86.2 26.8 %all-to-all-start.2 = ((f32[16,4,1280]{2,1,0:T(4,128)}), f32[16,4,1280]{2,1,0:T(4,128)S(1)}, u32[]{:S(2)}, u32[]{:S(2)}) async-start(f32[16,4,1280]{2,1,0:T(4,128)} %broadcast_in_dim.26), calls=%async_computation.2 | async-start | bytes 655360 | tf_op jit(solution)/shard_map/all_to_all | solution.py:29
  113.1 24.8 %copy-start.2 = (f32[16,256]{1,0:T(8,128)S(1)}, f32[16,256]{1,0:T(8,128)}, u32[]{:S(2)}) copy-start(f32[16,256]{1,0:T(8,128)} %param.11) | copy-start | bytes 49156
  115.9 9.6 %collective-permute-start.2 = (f32[256,256]{1,0:T(8,128)S(1)}, f32[256,256]{1,0:T(8,128)S(1)}, u32[]{:S(2)}, u32[]{:S(2)}) collective-permute-start(f32[256,256]{1,0:T(8,128)S(1)} %fusion.13), channel_id=1, source_target_pairs={{0,1},{1,0},{2,3},{3,2},{4,5},{5,4},{6,7},{7,6},{8,9},{9,8},{10,11... | collective-permute-start | bytes 786440 | tf_op jit(solution)/shard_map/ppermute | solution.py:25

commit v3 on v1

v3 whole, which is shorter than its diff:
```python
import jax
import jax.numpy as jnp
from jax import lax
from jax.sharding import Mesh
from jax.sharding import PartitionSpec as P

PLANE = ("y", "x")
LINE = "z"
CORE = "core"
CENTRE = ("z", "core")
EVERY = ("y", "x", "z", "core")


def product(left, right, left_dim, right_dim, precision=lax.Precision.HIGH):
    return lax.dot_general(
        left,
        right,
        (((left_dim,), (right_dim,)), ((), ())),
        precision=precision,
        preferred_element_type=jnp.float32,
    )


def swapped(value):
    return lax.ppermute(value, CORE, [(0, 1), (1, 0)])


def exchanged(blocks, axis):
    return lax.all_to_all(blocks, axis, split_axis=0, concat_axis=0, tiled=True)


def to_all(value, axis):
    return exchanged(jnp.broadcast_to(value, (lax.axis_size(axis), *value.shape)), axis)


def on_device(pool, sample_index, targets, centres, coeffs, eigvecs, eigscale):
    n_plane = lax.axis_size(PLANE)
    n_line = lax.axis_size(LINE)
    n_core = lax.axis_size(CORE)
    own, width = centres.shape
    rows = sample_index.shape[0]
    half = rows // n_core
    outs = coeffs.shape[1]
    total_centres = own * n_plane * n_line * n_core
    total_rows = rows * n_plane
    core = lax.axis_index(CORE)

    merged = jnp.concatenate([centres, coeffs, eigvecs], axis=1)
    group = to_all(merged, PLANE).reshape(own * n_plane, -1)

    chosen = lax.broadcasted_iota(jnp.int32, (pool.shape[0], rows), 0) == sample_index[None, :]
    picked = product(pool, chosen.astype(jnp.float32), 0, 0, lax.Precision.HIGHEST)
    batch_t = lax.all_gather(picked, CENTRE, axis=0, tiled=True)
    group, batch_t = lax.optimization_barrier((group, batch_t))

    zrows, terms = group[:, :width], group[:, width:]
    kernel = jnp.exp(product(batch_t, zrows, 0, 1) * (1.0 / jnp.sqrt(jnp.float32(width))))

    give = product(lax.dynamic_slice_in_dim(kernel, (1 - core) * half, half, 0), terms, 1, 0)
    come = swapped(give)
    part = product(lax.dynamic_slice_in_dim(kernel, core * half, half, 0), terms, 1, 0) + come
    tall, wide = 8, part.shape[1] * half // 8 // n_line
    across = part.shape[1] // wide
    blocks = part.reshape(half // tall, tall, across, wide).transpose(0, 2, 1, 3)
    own_sum = exchanged(blocks.reshape(n_line, tall, wide), LINE).sum(axis=0)
    whole = lax.all_gather(own_sum, CENTRE, axis=0)
    whole = whole.reshape(half // tall, across, n_core, tall, wide).transpose(2, 0, 3, 1, 4)
    whole = whole.reshape(rows, -1)

    model_norm = 1.0 / jnp.sqrt(jnp.float32(total_centres))
    residual = whole[:, :outs] * model_norm - targets
    scaled = whole[:, outs:] * eigscale
    weight = kernel - product(scaled, terms[:, outs:], 1, 1)
    change = product(weight, residual, 0, 0)
    change = exchanged(change.reshape(n_plane, own, outs), PLANE).sum(axis=0)
    step_size = 0.5 * jnp.sqrt(jnp.float32(total_centres) / jnp.float32(total_rows))
    return coeffs - (step_size * model_norm) * change


def solution(mesh):
    finer = Mesh(mesh.devices.reshape(4, 4, 16, 2), EVERY)
    placed = (
        P(PLANE, CENTRE),
        P(PLANE),
        P(PLANE, None),
        P(EVERY, None),
        P(EVERY, None),
        P(EVERY, None),
        P(),
    )
    return jax.shard_map(
        on_device, mesh=finer, in_specs=placed, out_specs=P(EVERY, None), check_vma=False
    )
```

time: 160 us -> 135 us (0.84)
  starting transfers between devices: 27.1 us -> 9.79 us
  blocking collectives: 101 us -> 117 us
  waiting for transfers between devices: 16.4 us -> 1.44 us
  matrix products: 10.6 us -> 2.72 us
    all_gather x0 -> x2, blocking collectives: none -> 77.4 us  [the longest x1 39 us: on_device(): whole = lax.all_gather(own_sum, CENTRE, axis=0)]
    all_to_all x4 -> x2, blocking collectives: 101 us -> 39.2 us  [exchanged(): return lax.all_to_all(blocks, axis, split_axis=0, concat_axis=0, tiled=True)]
    all_to_all x1, waiting for transfers between devices: 15.1 us -> 0.01 us  [exchanged(): return lax.all_to_all(blocks, axis, split_axis=0, concat_axis=0, tiled=True)]
    ppermute x3 -> x1, starting transfers between devices: 15.5 us -> 2.07 us  [swapped(): return lax.ppermute(value, CORE, [(0, 1), (1, 0)])]
    dot_general x8 -> x6, matrix products: 10.6 us -> 2.72 us  [product(): lax.dot_general(left, right, (((left_dim,), (right_dim,)), ((), ())), pre...]
    all_to_all x1, starting transfers between devices: 11.6 us -> 7.72 us  [exchanged(): return lax.all_to_all(blocks, axis, split_axis=0, concat_axis=0, tiled=True)]
  transfers between devices with their start and end apart: 4 -> 2, of which waited for: 3 -> 1; matrix products, arithmetic and copies ran while one was open for 3% -> 0% of each run, Pallas kernels for 0% -> 0%
where the time goes in v3:
time: 135 us; the launch traced here: 134 us
  blocking collectives  117 us (87%)
  starting transfers between devices  9.79 us (7%)
  matrix products  2.72 us (2%)
  local copies, waits for them, and re-layouts  2.05 us (2%)
  other arithmetic  1.56 us (1%)
  waiting for transfers between devices  1.44 us (1%)
    all_to_all x2, blocking collectives, exchanged(): return lax.all_to_all(blocks, axis, split_axis=0, concat_axis=0, tiled=True)  39.2 us
    all_gather x1, blocking collectives, on_device(): whole = lax.all_gather(own_sum, CENTRE, axis=0)  39 us
    all_gather x1, blocking collectives, on_device(): batch_t = lax.all_gather(picked, CENTRE, axis=0, tiled=True)  38.5 us
    all_to_all x1, starting transfers between devices, exchanged(): return lax.all_to_all(blocks, axis, split_axis=0, concat_axis=0, tiled=True)  7.72 us
    dot_general x6, matrix products, product(): lax.dot_general(left, right, (((left_dim,), (right_dim,)), ((), ())), pre...  2.72 us
  transfers between devices with their start and end apart: 2, of which 1 were waited for; matrix products, arithmetic and copies ran while one was open for 0% of the time, Pallas kernels for 0%

profile of v3, /device:TPU:1, one launch (start us, length us, event | category | flops | bytes accessed | tf_op | source)
XLA Modules:
  0.0 134.4 jit_solution(8380901534712084741)
XLA Ops:
  0.0 0.0 copy-start
  0.0 0.9 pad_maximum_fusion
  0.9 1.6 %broadcast_in_dim.2 = f32[16,16,2304]{2,1,0:T(8,128)} broadcast(f32[16,2304]{1,0:T(8,128)S(1)} %pad_maximum_fusion), dimensions={1,2} | broadcast | bytes 2506752 | tf_op jit(solution)/shard_map/broadcast_in_dim | solution.py:33
  2.6 7.7 %all-to-all-start = ((f32[16,16,2304]{2,1,0:T(8,128)}), f32[16,16,2304]{2,1,0:T(8,128)S(1)}, u32[]{:S(2)}, u32[]{:S(2)}) async-start(f32[16,16,2304]{2,1,0:T(8,128)} %broadcast_in_dim.2), calls=%async_computation | async-start | bytes 4718592 | tf_op jit(solution)/shard_map/all_to_all | solution.py:29
  10.3 0.0 copy-done
  10.3 0.0 copy-done.4
  10.3 0.2 convolution_bitcast_fusion
  10.5 38.5 %all_gather.9 = f32[1024,128]{1,0:T(8,128)S(1)} all-gather(f32[32,128]{1,0:T(8,128)S(1)} %convolution_bitcast_fusion), channel_id=1, replica_groups=mesh['y'=4,'x'=4,'z'=16,'core'=2] {'z','core'}, dimensions={0}, use_global_device_ids=true | all-gather | bytes 540672 | tf_op jit(solution)/shard_map/all_gather | solution.py:53
  48.9 0.0 all-to-all-done
  48.9 0.6 fusion.3
  49.5 0.5 fusion
  50.0 2.1 %collective-permute-start = (f32[64,1280]{1,0:T(8,128)S(1)}, f32[64,1280]{1,0:T(8,128)S(1)}, u32[]{:S(2)}, u32[]{:S(2)}) collective-permute-start(f32[64,1280]{1,0:T(8,128)S(1)} %fusion), channel_id=1, source_target_pairs={{0,1},{1,0},{2,3},{3,2},{4,5},{5,4},{6,7},{7,6},{8,9},{9,8},{10,11... | collective-permute-start | bytes 983048 | tf_op jit(solution)/shard_map/ppermute | solution.py:25
  52.1 1.4 %collective-permute-done = f32[64,1280]{1,0:T(8,128)S(1)} collective-permute-done((f32[64,1280]{1,0:T(8,128)S(1)}, f32[64,1280]{1,0:T(8,128)S(1)}, u32[]{:S(2)}, u32[]{:S(2)}) %collective-permute-start) | collective-permute-done | bytes 327712 | tf_op jit(solution)/shard_map/ppermute | solution.py:25
  53.6 0.5 convolution_add_fusion
  54.1 0.0 copy-start.3
  54.1 27.5 %all_to_all.15 = f32[16,8,640]{2,1,0:T(8,128)S(1)} all-to-all(f32[16,8,640]{2,1,0:T(8,128)S(1)} %bitcast.26), channel_id=1, replica_groups=mesh['y'=4,'x'=4,'z'=16,'core'=2] {'z'}, dimensions={0} | all-to-all | bytes 655360 | tf_op jit(solution)/shard_map/all_to_all | solution.py:29
  81.7 39.0 %all-gather = f32[256,640]{1,0:T(8,128)S(1)} all-gather(f32[8,640]{1,0:T(8,128)S(1)} %reduce_sum.18), channel_id=2, replica_groups=mesh['y'=4,'x'=4,'z'=16,'core'=2] {'z','core'}, dimensions={0}, use_global_device_ids=true | all-gather | bytes 675840 | tf_op jit(solution)/shard_map/all_gather | solution.py:66
  120.6 0.3 copy.8
  121.0 0.0 copy-start.2
  121.0 0.0 copy-done.3
  121.1 0.7 convolution_subtract_fusion
  121.7 0.3 fusion.8
  122.1 11.7 %all_to_all.16 = f32[16,16,256]{2,1,0:T(8,128)S(1)} all-to-all(f32[16,16,256]{2,1,0:T(8,128)S(1)} %bitcast.27), channel_id=1, replica_groups=mesh['y'=4,'x'=4,'z'=16,'core'=2] {'y','x'}, dimensions={0} | all-to-all | bytes 524288 | tf_op jit(solution)/shard_map/all_to_all | solution.py:29
  133.8 0.6 multiply_subtract_fusion
  (7 shorter events, 0.1 us)
Async XLA Ops:
  0.0 10.3 %copy-start = (f32[256,32]{0,1:T(8,128)S(1)}, f32[256,32]{0,1:T(8,128)}, u32[]{:S(2)}) copy-start(f32[256,32]{0,1:T(8,128)} %param.7) | copy-start | bytes 98308
  2.6 7.7 %copy-start.4 = (s32[128]{0:T(128)S(1)}, s32[128]{0:T(128)}, u32[]{:S(2)}) copy-start(s32[128]{0:T(128)} %param.8) | copy-start | bytes 1540
  2.6 46.4 %all-to-all-start = ((f32[16,16,2304]{2,1,0:T(8,128)}), f32[16,16,2304]{2,1,0:T(8,128)S(1)}, u32[]{:S(2)}, u32[]{:S(2)}) async-start(f32[16,16,2304]{2,1,0:T(8,128)} %broadcast_in_dim.2), calls=%async_computation | async-start | bytes 4718592 | tf_op jit(solution)/shard_map/all_to_all | solution.py:29
  50.0 3.5 %collective-permute-start = (f32[64,1280]{1,0:T(8,128)S(1)}, f32[64,1280]{1,0:T(8,128)S(1)}, u32[]{:S(2)}, u32[]{:S(2)}) collective-permute-start(f32[64,1280]{1,0:T(8,128)S(1)} %fusion), channel_id=1, source_target_pairs={{0,1},{1,0},{2,3},{3,2},{4,5},{5,4},{6,7},{7,6},{8,9},{9,8},{10,11... | collective-permute-start | bytes 983048 | tf_op jit(solution)/shard_map/ppermute | solution.py:25
  54.1 67.0 %copy-start.3 = (f32[1024]{0:T(1024)S(1)}, f32[1024]{0:T(1024)}, u32[]{:S(2)}) copy-start(f32[1024]{0:T(1024)} %param.13) | copy-start | bytes 12292
  120.6 1.1 copy-start.1
  121.0 12.8 %copy-start.2 = (f32[16,256]{1,0:T(8,128)S(1)}, f32[16,256]{1,0:T(8,128)}, u32[]{:S(2)}) copy-start(f32[16,256]{1,0:T(8,128)} %param.11) | copy-start | bytes 49156

commit v4 on v3

--- a/solution.py
+++ b/solution.py
@@ -5,10 +5,12 @@
 from jax.sharding import PartitionSpec as P
 
 PLANE = ("y", "x")
-LINE = "z"
+FAR = "z_far"
+NEAR = "z_near"
 CORE = "core"
-CENTRE = ("z", "core")
-EVERY = ("y", "x", "z", "core")
+NEAR_CORE = ("z_near", "core")
+CENTRE = ("z_far", "z_near", "core")
+EVERY = ("y", "x", "z_far", "z_near", "core")
 
 
 def product(left, right, left_dim, right_dim, precision=lax.Precision.HIGH):
@@ -35,13 +37,12 @@
 
 def on_device(pool, sample_index, targets, centres, coeffs, eigvecs, eigscale):
     n_plane = lax.axis_size(PLANE)
-    n_line = lax.axis_size(LINE)
+    n_near = lax.axis_size(NEAR)
     n_core = lax.axis_size(CORE)
     own, width = centres.shape
     rows = sample_index.shape[0]
-    half = rows // n_core
     outs = coeffs.shape[1]
-    total_centres = own * n_plane * n_line * n_core
+    total_centres = own * n_plane * lax.axis_size(CENTRE)
     total_rows = rows * n_plane
     core = lax.axis_index(CORE)
 
@@ -56,16 +57,17 @@
     zrows, terms = group[:, :width], group[:, width:]
     kernel = jnp.exp(product(batch_t, zrows, 0, 1) * (1.0 / jnp.sqrt(jnp.float32(width))))
 
-    give = product(lax.dynamic_slice_in_dim(kernel, (1 - core) * half, half, 0), terms, 1, 0)
-    come = swapped(give)
-    part = product(lax.dynamic_slice_in_dim(kernel, core * half, half, 0), terms, 1, 0) + come
-    tall, wide = 8, part.shape[1] * half // 8 // n_line
-    across = part.shape[1] // wide
-    blocks = part.reshape(half // tall, tall, across, wide).transpose(0, 2, 1, 3)
-    own_sum = exchanged(blocks.reshape(n_line, tall, wide), LINE).sum(axis=0)
-    whole = lax.all_gather(own_sum, CENTRE, axis=0)
-    whole = whole.reshape(half // tall, across, n_core, tall, wide).transpose(2, 0, 3, 1, 4)
-    whole = whole.reshape(rows, -1)
+    tall = rows // (n_near * n_core)
+    by_core = kernel.reshape(n_near, n_core, tall, -1)
+
+    def term_sums(of_core):
+        taken = lax.dynamic_index_in_dim(by_core, of_core, 1, keepdims=False)
+        return product(taken.reshape(rows // n_core, -1), terms, 1, 0)
+
+    part = swapped(term_sums(1 - core)) + term_sums(core)
+    near_sum = exchanged(part.reshape(n_near, tall, -1), NEAR).sum(axis=0)
+    own_sum = lax.all_gather(near_sum, FAR, axis=0).sum(axis=0)
+    whole = lax.all_gather(own_sum, NEAR_CORE, axis=0, tiled=True)
 
     model_norm = 1.0 / jnp.sqrt(jnp.float32(total_centres))
     residual = whole[:, :outs] * model_norm - targets
@@ -78,7 +80,7 @@
 
 
 def solution(mesh):
-    finer = Mesh(mesh.devices.reshape(4, 4, 16, 2), EVERY)
+    finer = Mesh(mesh.devices.reshape(4, 4, 4, 4, 2), EVERY)
     placed = (
         P(PLANE, CENTRE),
         P(PLANE),

time: 135 us -> 125 us (0.926)
  blocking collectives: 117 us -> 108 us
    all_to_all x2, blocking collectives: 39.2 us -> 24.3 us  [exchanged(): return lax.all_to_all(blocks, axis, split_axis=0, concat_axis=0, tiled=True)]
    all_gather x1 -> x2, blocking collectives: 39 us -> 44.9 us  [the longest x1 23.8 us: on_device(): own_sum = lax.all_gather(near_sum, FAR, axis=0).sum(axis=0)]
where the time goes in v4:
time: 125 us
  blocking collectives  108 us (86%)
  starting transfers between devices  9.79 us (8%)
  matrix products  2.72 us (2%)
  local copies, waits for them, and re-layouts  1.68 us (1%)
  other arithmetic  1.58 us (1%)
  waiting for transfers between devices  1.45 us (1%)
    all_gather x1, blocking collectives, on_device(): batch_t = lax.all_gather(picked, CENTRE, axis=0, tiled=True)  38.5 us
    all_to_all x2, blocking collectives, exchanged(): return lax.all_to_all(blocks, axis, split_axis=0, concat_axis=0, tiled=True)  24.3 us
    all_gather x1, blocking collectives, on_device(): own_sum = lax.all_gather(near_sum, FAR, axis=0).sum(axis=0)  23.8 us
    all_gather x1, blocking collectives, on_device(): whole = lax.all_gather(own_sum, NEAR_CORE, axis=0, tiled=True)  21 us
    all_to_all x1, starting transfers between devices, exchanged(): return lax.all_to_all(blocks, axis, split_axis=0, concat_axis=0, tiled=True)  7.72 us
    dot_general x6, matrix products, product(): lax.dot_general(left, right, (((left_dim,), (right_dim,)), ((), ())), pre...  2.72 us
  transfers between devices with their start and end apart: 2, of which 1 were waited for; matrix products, arithmetic and copies ran while one was open for 0% of the time, Pallas kernels for 0%

profile of v4, /device:TPU:1, one launch (start us, length us, event | category | flops | bytes accessed | tf_op | source)
XLA Modules:
  0.0 125.0 jit_solution(10646864156142121993)
XLA Ops:
  0.0 0.9 pad_maximum_fusion
  0.9 1.6 %broadcast_in_dim.2 = f32[16,16,2304]{2,1,0:T(8,128)} broadcast(f32[16,2304]{1,0:T(8,128)S(1)} %pad_maximum_fusion), dimensions={1,2} | broadcast | bytes 2506752 | tf_op jit(solution)/shard_map/broadcast_in_dim | solution.py:35
  2.6 7.7 %all-to-all-start = ((f32[16,16,2304]{2,1,0:T(8,128)}), f32[16,16,2304]{2,1,0:T(8,128)S(1)}, u32[]{:S(2)}, u32[]{:S(2)}) async-start(f32[16,16,2304]{2,1,0:T(8,128)} %broadcast_in_dim.2), calls=%async_computation | async-start | bytes 4718592 | tf_op jit(solution)/shard_map/all_to_all | solution.py:31
  10.3 0.0 copy-done
  10.3 0.0 copy-done.4
  10.3 0.2 convolution_bitcast_fusion
  10.5 38.5 %all_gather.12 = f32[1024,128]{1,0:T(8,128)S(1)} all-gather(f32[32,128]{1,0:T(8,128)S(1)} %convolution_bitcast_fusion), channel_id=1, replica_groups=mesh['y'=4,'x'=4,'z_far'=4,'z_near'=4,'core'=2] {'z_far','z_near','core'}, dimensions={0}, use_global_device_ids=true | all-gather | bytes 540672 | tf_op jit(solution)/shard_map/all_gather | solution.py:54
  48.9 0.0 all-to-all-done
  48.9 0.6 fusion.3
  49.6 0.5 fusion.1
  50.1 0.0 copy-start.3
  50.1 2.1 %collective-permute-start = (f32[64,1280]{1,0:T(8,128)S(1)}, f32[64,1280]{1,0:T(8,128)S(1)}, u32[]{:S(2)}, u32[]{:S(2)}) collective-permute-start(f32[64,1280]{1,0:T(8,128)S(1)} %fusion.1), channel_id=1, source_target_pairs={{0,1},{1,0},{2,3},{3,2},{4,5},{5,4},{6,7},{7,6},{8,9},{9,8},{10,11... | collective-permute-start | bytes 983048 | tf_op jit(solution)/shard_map/ppermute | solution.py:27
  52.1 1.4 %collective-permute-done = f32[64,1280]{1,0:T(8,128)S(1)} collective-permute-done((f32[64,1280]{1,0:T(8,128)S(1)}, f32[64,1280]{1,0:T(8,128)S(1)}, u32[]{:S(2)}, u32[]{:S(2)}) %collective-permute-start) | collective-permute-done | bytes 327712 | tf_op jit(solution)/shard_map/ppermute | solution.py:27
  53.6 0.5 convolution_add_fusion
  54.1 0.0 copy-start.1
  54.1 12.6 %all_to_all.15 = f32[4,16,1280]{2,1,0:T(8,128)S(1)} all-to-all(f32[4,16,1280]{2,1,0:T(8,128)S(1)} %bitcast.18), channel_id=1, replica_groups=mesh['y'=4,'x'=4,'z_far'=4,'z_near'=4,'core'=2] {'z_near'}, dimensions={0} | all-to-all | bytes 655360 | tf_op jit(solution)/shard_map/all_to_all | solution.py:31
  66.7 0.0 copy-start.2
  66.8 23.8 %all-gather = f32[64,1280]{1,0:T(8,128)S(1)} all-gather(f32[16,1280]{1,0:T(8,128)S(1)} %reduce_sum.27), channel_id=2, replica_groups=mesh['y'=4,'x'=4,'z_far'=4,'z_near'=4,'core'=2] {'z_far'}, dimensions={0}, use_global_device_ids=true | all-gather | bytes 409600 | tf_op jit(solution)/shard_map/all_gather | solution.py:69
  90.6 21.0 %all_gather.15 = f32[128,1280]{1,0:T(8,128)S(1)} all-gather(f32[16,1280]{1,0:T(8,128)S(1)} %reduce_sum.28), channel_id=1, replica_groups=mesh['y'=4,'x'=4,'z_far'=4,'z_near'=4,'core'=2] {'z_near','core'}, dimensions={0}, use_global_device_ids=true | all-gather | bytes 737280 | tf_op jit(solution)/shard_map/all_gather | solution.py:70
  111.7 0.7 convolution_subtract_fusion
  112.3 0.3 fusion.8
  112.7 11.7 %all_to_all.16 = f32[16,16,256]{2,1,0:T(8,128)S(1)} all-to-all(f32[16,16,256]{2,1,0:T(8,128)S(1)} %bitcast.21), channel_id=1, replica_groups=mesh['y'=4,'x'=4,'z_far'=4,'z_near'=4,'core'=2] {'y','x'}, dimensions={0} | all-to-all | bytes 524288 | tf_op jit(solution)/shard_map/all_to_all | solution.py:31
  124.3 0.0 copy-done.2
  124.4 0.6 multiply_subtract_fusion
  (8 shorter events, 0.1 us)
Async XLA Ops:
  0.0 10.3 %copy-start = (f32[256,32]{0,1:T(8,128)S(1)}, f32[256,32]{0,1:T(8,128)}, u32[]{:S(2)}) copy-start(f32[256,32]{0,1:T(8,128)} %param.7) | copy-start | bytes 98308
  2.5 7.7 %copy-start.4 = (s32[128]{0:T(128)S(1)}, s32[128]{0:T(128)}, u32[]{:S(2)}) copy-start(s32[128]{0:T(128)} %param.8) | copy-start | bytes 1540
  2.6 46.4 %all-to-all-start = ((f32[16,16,2304]{2,1,0:T(8,128)}), f32[16,16,2304]{2,1,0:T(8,128)S(1)}, u32[]{:S(2)}, u32[]{:S(2)}) async-start(f32[16,16,2304]{2,1,0:T(8,128)} %broadcast_in_dim.2), calls=%async_computation | async-start | bytes 4718592 | tf_op jit(solution)/shard_map/all_to_all | solution.py:31
  50.1 61.6 %copy-start.3 = (f32[1024]{0:T(1024)S(1)}, f32[1024]{0:T(1024)}, u32[]{:S(2)}) copy-start(f32[1024]{0:T(1024)} %param.13) | copy-start | bytes 12292
  50.1 3.5 %collective-permute-start = (f32[64,1280]{1,0:T(8,128)S(1)}, f32[64,1280]{1,0:T(8,128)S(1)}, u32[]{:S(2)}, u32[]{:S(2)}) collective-permute-start(f32[64,1280]{1,0:T(8,128)S(1)} %fusion.1), channel_id=1, source_target_pairs={{0,1},{1,0},{2,3},{3,2},{4,5},{5,4},{6,7},{7,6},{8,9},{9,8},{10,11... | collective-permute-start | bytes 983048 | tf_op jit(solution)/shard_map/ppermute | solution.py:27
  54.1 58.2 %copy-start.1 = (f32[128,256]{1,0:T(8,128)S(1)}, f32[128,256]{1,0:T(8,128)}, u32[]{:S(2)}) copy-start(f32[128,256]{1,0:T(8,128)} %param.9) | copy-start | bytes 393220
  66.7 57.6 %copy-start.2 = (f32[16,256]{1,0:T(8,128)S(1)}, f32[16,256]{1,0:T(8,128)}, u32[]{:S(2)}) copy-start(f32[16,256]{1,0:T(8,128)} %param.11) | copy-start | bytes 49156

commit v5 on v4

--- a/solution.py
+++ b/solution.py
@@ -4,13 +4,14 @@
 from jax.sharding import Mesh
 from jax.sharding import PartitionSpec as P
 
-PLANE = ("y", "x")
+PLANE = "plane"
+ORDER = [[2, 12, 0, 14, 1, 5, 3, 7, 10, 4, 8, 6, 9, 13, 11, 15]]
 FAR = "z_far"
 NEAR = "z_near"
 CORE = "core"
 NEAR_CORE = ("z_near", "core")
 CENTRE = ("z_far", "z_near", "core")
-EVERY = ("y", "x", "z_far", "z_near", "core")
+EVERY = ("plane", "z_far", "z_near", "core")
 
 
 def product(left, right, left_dim, right_dim, precision=lax.Precision.HIGH):
@@ -27,12 +28,14 @@
     return lax.ppermute(value, CORE, [(0, 1), (1, 0)])
 
 
-def exchanged(blocks, axis):
-    return lax.all_to_all(blocks, axis, split_axis=0, concat_axis=0, tiled=True)
+def exchanged(blocks, axis, groups=None):
+    return lax.all_to_all(
+        blocks, axis, split_axis=0, concat_axis=0, axis_index_groups=groups, tiled=True
+    )
 
 
-def to_all(value, axis):
-    return exchanged(jnp.broadcast_to(value, (lax.axis_size(axis), *value.shape)), axis)
+def to_all(value, axis, groups=None):
+    return exchanged(jnp.broadcast_to(value, (lax.axis_size(axis), *value.shape)), axis, groups)
 
 
 def on_device(pool, sample_index, targets, centres, coeffs, eigvecs, eigscale):
@@ -47,7 +50,7 @@
     core = lax.axis_index(CORE)
 
     merged = jnp.concatenate([centres, coeffs, eigvecs], axis=1)
-    group = to_all(merged, PLANE).reshape(own * n_plane, -1)
+    group = to_all(merged, PLANE, ORDER).reshape(own * n_plane, -1)
 
     chosen = lax.broadcasted_iota(jnp.int32, (pool.shape[0], rows), 0) == sample_index[None, :]
     picked = product(pool, chosen.astype(jnp.float32), 0, 0, lax.Precision.HIGHEST)
@@ -74,13 +77,13 @@
     scaled = whole[:, outs:] * eigscale
     weight = kernel - product(scaled, terms[:, outs:], 1, 1)
     change = product(weight, residual, 0, 0)
-    change = exchanged(change.reshape(n_plane, own, outs), PLANE).sum(axis=0)
+    change = exchanged(change.reshape(n_plane, own, outs), PLANE, ORDER).sum(axis=0)
     step_size = 0.5 * jnp.sqrt(jnp.float32(total_centres) / jnp.float32(total_rows))
     return coeffs - (step_size * model_norm) * change
 
 
 def solution(mesh):
-    finer = Mesh(mesh.devices.reshape(4, 4, 4, 4, 2), EVERY)
+    finer = Mesh(mesh.devices.reshape(16, 4, 4, 2), EVERY)
     placed = (
         P(PLANE, CENTRE),
         P(PLANE),

time: 125 us -> 121 us (0.968)
  blocking collectives: 108 us -> 102 us
    all_gather x1, blocking collectives: 23.8 us -> 17.9 us  [on_device(): own_sum = lax.all_gather(near_sum, FAR, axis=0).sum(axis=0)]
    all_to_all x2, blocking collectives: 24.3 us -> 25.6 us  [exchanged(): lax.all_to_all(blocks, axis, split_axis=0, concat_axis=0, axis_index_grou...]
where the time goes in v5:
time: 121 us; the launch traced here: 120 us
  blocking collectives  102 us (84%)
  starting transfers between devices  10.6 us (9%)
  matrix products  2.71 us (2%)
  local copies, waits for them, and re-layouts  1.68 us (1%)
  other arithmetic  1.58 us (1%)
  waiting for transfers between devices  1.44 us (1%)
    all_gather x1, blocking collectives, on_device(): batch_t = lax.all_gather(picked, CENTRE, axis=0, tiled=True)  38.7 us
    all_to_all x2, blocking collectives, exchanged(): lax.all_to_all(blocks, axis, split_axis=0, concat_axis=0, axis_index_grou...  25.6 us
    all_gather x1, blocking collectives, on_device(): whole = lax.all_gather(own_sum, NEAR_CORE, axis=0, tiled=True)  19.9 us
    all_gather x1, blocking collectives, on_device(): own_sum = lax.all_gather(near_sum, FAR, axis=0).sum(axis=0)  17.9 us
    all_to_all x1, starting transfers between devices, exchanged(): lax.all_to_all(blocks, axis, split_axis=0, concat_axis=0, axis_index_grou...  8.54 us
    dot_general x6, matrix products, product(): lax.dot_general(left, right, (((left_dim,), (right_dim,)), ((), ())), pre...  2.71 us
  transfers between devices with their start and end apart: 2, of which 1 were waited for; matrix products, arithmetic and copies ran while one was open for 0% of the time, Pallas kernels for 0%

profile of v5, /device:TPU:1, one launch (start us, length us, event | category | flops | bytes accessed | tf_op | source)
XLA Modules:
  0.0 120.3 jit_solution(16719609503165119980)
XLA Ops:
  0.0 0.0 copy-start
  0.0 0.9 pad_maximum_fusion
  0.9 1.6 %broadcast_in_dim.2 = f32[16,16,2304]{2,1,0:T(8,128)} broadcast(f32[16,2304]{1,0:T(8,128)S(1)} %pad_maximum_fusion), dimensions={1,2} | broadcast | bytes 2506752 | tf_op jit(solution)/shard_map/broadcast_in_dim | solution.py:38
  2.6 8.5 %all-to-all-start = ((f32[16,16,2304]{2,1,0:T(8,128)}), f32[16,16,2304]{2,1,0:T(8,128)S(1)}, u32[]{:S(2)}, u32[]{:S(2)}) async-start(f32[16,16,2304]{2,1,0:T(8,128)} %broadcast_in_dim.2), calls=%async_computation | async-start | bytes 4718592 | tf_op jit(solution)/shard_map/all_to_all | solution.py:32
  11.1 0.0 copy-done
  11.1 0.0 copy-done.4
  11.1 0.2 convolution_bitcast_fusion
  11.3 38.7 %all_gather.12 = f32[1024,128]{1,0:T(8,128)S(1)} all-gather(f32[32,128]{1,0:T(8,128)S(1)} %convolution_bitcast_fusion), channel_id=1, replica_groups=mesh['plane'=16,'z_far'=4,'z_near'=4,'core'=2] {'z_far','z_near','core'}, dimensions={0}, use_global_device_ids=true | all-gather | bytes 540672 | tf_op jit(solution)/shard_map/all_gather | solution.py:57
  50.0 0.0 all-to-all-done
  50.0 0.6 fusion.3
  50.6 0.5 fusion.1
  51.1 0.0 copy-start.3
  51.2 2.1 %collective-permute-start = (f32[64,1280]{1,0:T(8,128)S(1)}, f32[64,1280]{1,0:T(8,128)S(1)}, u32[]{:S(2)}, u32[]{:S(2)}) collective-permute-start(f32[64,1280]{1,0:T(8,128)S(1)} %fusion.1), channel_id=1, source_target_pairs={{0,1},{1,0},{2,3},{3,2},{4,5},{5,4},{6,7},{7,6},{8,9},{9,8},{10,11... | collective-permute-start | bytes 983048 | tf_op jit(solution)/shard_map/ppermute | solution.py:28
  53.2 1.4 %collective-permute-done = f32[64,1280]{1,0:T(8,128)S(1)} collective-permute-done((f32[64,1280]{1,0:T(8,128)S(1)}, f32[64,1280]{1,0:T(8,128)S(1)}, u32[]{:S(2)}, u32[]{:S(2)}) %collective-permute-start) | collective-permute-done | bytes 327712 | tf_op jit(solution)/shard_map/ppermute | solution.py:28
  54.7 0.5 convolution_add_fusion
  55.2 0.0 copy-start.1
  55.2 12.8 %all_to_all.15 = f32[4,16,1280]{2,1,0:T(8,128)S(1)} all-to-all(f32[4,16,1280]{2,1,0:T(8,128)S(1)} %bitcast.18), channel_id=1, replica_groups=mesh['plane'=16,'z_far'=4,'z_near'=4,'core'=2] {'z_near'}, dimensions={0} | all-to-all | bytes 655360 | tf_op jit(solution)/shard_map/all_to_all | solution.py:32
  68.0 0.0 copy-start.2
  68.0 17.9 %all-gather = f32[64,1280]{1,0:T(8,128)S(1)} all-gather(f32[16,1280]{1,0:T(8,128)S(1)} %reduce_sum.27), channel_id=2, replica_groups=mesh['plane'=16,'z_far'=4,'z_near'=4,'core'=2] {'z_far'}, dimensions={0}, use_global_device_ids=true | all-gather | bytes 409600 | tf_op jit(solution)/shard_map/all_gather | solution.py:72
  86.0 19.9 %all_gather.15 = f32[128,1280]{1,0:T(8,128)S(1)} all-gather(f32[16,1280]{1,0:T(8,128)S(1)} %reduce_sum.28), channel_id=1, replica_groups=mesh['plane'=16,'z_far'=4,'z_near'=4,'core'=2] {'z_near','core'}, dimensions={0}, use_global_device_ids=true | all-gather | bytes 737280 | tf_op jit(solution)/shard_map/all_gather | solution.py:73
  105.8 0.7 convolution_subtract_fusion
  106.5 0.3 fusion.8
  106.8 12.9 %all_to_all.16 = f32[16,16,256]{2,1,0:T(8,128)S(1)} all-to-all(f32[16,16,256]{2,1,0:T(8,128)S(1)} %bitcast.21), channel_id=1, replica_groups={{64,384,0,448,32,160,96,224,320,128,256,192,288,416,352,480},{65,385,1,..., dimensions={0} | all-to-all | bytes 524288 | tf_op jit(solution)/shard_map/all_to_all | solution.py:32
  119.7 0.6 multiply_subtract_fusion
  (8 shorter events, 0.1 us)
Async XLA Ops:
  0.0 11.1 %copy-start = (f32[256,32]{0,1:T(8,128)S(1)}, f32[256,32]{0,1:T(8,128)}, u32[]{:S(2)}) copy-start(f32[256,32]{0,1:T(8,128)} %param.7) | copy-start | bytes 98308
  2.5 8.6 %copy-start.4 = (s32[128]{0:T(128)S(1)}, s32[128]{0:T(128)}, u32[]{:S(2)}) copy-start(s32[128]{0:T(128)} %param.8) | copy-start | bytes 1540
  2.6 47.5 %all-to-all-start = ((f32[16,16,2304]{2,1,0:T(8,128)}), f32[16,16,2304]{2,1,0:T(8,128)S(1)}, u32[]{:S(2)}, u32[]{:S(2)}) async-start(f32[16,16,2304]{2,1,0:T(8,128)} %broadcast_in_dim.2), calls=%async_computation | async-start | bytes 4718592 | tf_op jit(solution)/shard_map/all_to_all | solution.py:32
  51.1 54.7 %copy-start.3 = (f32[1024]{0:T(1024)S(1)}, f32[1024]{0:T(1024)}, u32[]{:S(2)}) copy-start(f32[1024]{0:T(1024)} %param.13) | copy-start | bytes 12292
  51.2 3.5 %collective-permute-start = (f32[64,1280]{1,0:T(8,128)S(1)}, f32[64,1280]{1,0:T(8,128)S(1)}, u32[]{:S(2)}, u32[]{:S(2)}) collective-permute-start(f32[64,1280]{1,0:T(8,128)S(1)} %fusion.1), channel_id=1, source_target_pairs={{0,1},{1,0},{2,3},{3,2},{4,5},{5,4},{6,7},{7,6},{8,9},{9,8},{10,11... | collective-permute-start | bytes 983048 | tf_op jit(solution)/shard_map/ppermute | solution.py:28
  55.2 51.3 %copy-start.1 = (f32[128,256]{1,0:T(8,128)S(1)}, f32[128,256]{1,0:T(8,128)}, u32[]{:S(2)}) copy-start(f32[128,256]{1,0:T(8,128)} %param.9) | copy-start | bytes 393220
  68.0 51.7 %copy-start.2 = (f32[16,256]{1,0:T(8,128)S(1)}, f32[16,256]{1,0:T(8,128)}, u32[]{:S(2)}) copy-start(f32[16,256]{1,0:T(8,128)} %param.11) | copy-start | bytes 49156

commit v6 on v5

--- a/solution.py
+++ b/solution.py
@@ -11,6 +11,8 @@
 CORE = "core"
 NEAR_CORE = ("z_near", "core")
 CENTRE = ("z_far", "z_near", "core")
+NEAR_ORDER = [[0, 1, 3, 2]]
+NEAR_CORE_ORDER = [[2 * near + core for near in NEAR_ORDER[0] for core in range(2)]]
 EVERY = ("plane", "z_far", "z_near", "core")
 
 
@@ -68,9 +70,11 @@
         return product(taken.reshape(rows // n_core, -1), terms, 1, 0)
 
     part = swapped(term_sums(1 - core)) + term_sums(core)
-    near_sum = exchanged(part.reshape(n_near, tall, -1), NEAR).sum(axis=0)
+    near_sum = exchanged(part.reshape(n_near, tall, -1), NEAR, NEAR_ORDER).sum(axis=0)
     own_sum = lax.all_gather(near_sum, FAR, axis=0).sum(axis=0)
-    whole = lax.all_gather(own_sum, NEAR_CORE, axis=0, tiled=True)
+    whole = lax.all_gather(
+        own_sum, NEAR_CORE, axis_index_groups=NEAR_CORE_ORDER, axis=0, tiled=True
+    )
 
     model_norm = 1.0 / jnp.sqrt(jnp.float32(total_centres))
     residual = whole[:, :outs] * model_norm - targets

time: 121 us -> 119 us (0.983)
  blocking collectives: 102 us -> 100 us
    all_gather x1, blocking collectives: 19.9 us -> 17.4 us  [on_device(): lax.all_gather(own_sum, NEAR_CORE, axis_index_groups=NEAR_CORE_ORDER, axi...]
where the time goes in v6:
time: 119 us; the launch traced here: 118 us
  blocking collectives  100 us (84%)
  starting transfers between devices  10.6 us (9%)
  matrix products  2.71 us (2%)
  local copies, waits for them, and re-layouts  1.68 us (1%)
  other arithmetic  1.58 us (1%)
  waiting for transfers between devices  1.44 us (1%)
    all_gather x1, blocking collectives, on_device(): batch_t = lax.all_gather(picked, CENTRE, axis=0, tiled=True)  38.7 us
    all_to_all x2, blocking collectives, exchanged(): lax.all_to_all(blocks, axis, split_axis=0, concat_axis=0, axis_index_grou...  26.1 us
    all_gather x1, blocking collectives, on_device(): own_sum = lax.all_gather(near_sum, FAR, axis=0).sum(axis=0)  17.8 us
    all_gather x1, blocking collectives, on_device(): lax.all_gather(own_sum, NEAR_CORE, axis_index_groups=NEAR_CORE_ORDER, axi...  17.4 us
    all_to_all x1, starting transfers between devices, exchanged(): lax.all_to_all(blocks, axis, split_axis=0, concat_axis=0, axis_index_grou...  8.54 us
    dot_general x6, matrix products, product(): lax.dot_general(left, right, (((left_dim,), (right_dim,)), ((), ())), pre...  2.71 us
  transfers between devices with their start and end apart: 2, of which 1 were waited for; matrix products, arithmetic and copies ran while one was open for 0% of the time, Pallas kernels for 0%

profile of v6, /device:TPU:1, one launch (start us, length us, event | category | flops | bytes accessed | tf_op | source)
XLA Modules:
  0.0 118.2 jit_solution(9920398992186220316)
XLA Ops:
  0.0 0.0 copy-start
  0.0 0.9 pad_maximum_fusion
  0.9 1.6 %broadcast_in_dim.2 = f32[16,16,2304]{2,1,0:T(8,128)} broadcast(f32[16,2304]{1,0:T(8,128)S(1)} %pad_maximum_fusion), dimensions={1,2} | broadcast | bytes 2506752 | tf_op jit(solution)/shard_map/broadcast_in_dim | solution.py:40
  2.6 8.5 %all-to-all-start = ((f32[16,16,2304]{2,1,0:T(8,128)}), f32[16,16,2304]{2,1,0:T(8,128)S(1)}, u32[]{:S(2)}, u32[]{:S(2)}) async-start(f32[16,16,2304]{2,1,0:T(8,128)} %broadcast_in_dim.2), calls=%async_computation | async-start | bytes 4718592 | tf_op jit(solution)/shard_map/all_to_all | solution.py:34
  11.1 0.2 convolution_bitcast_fusion
  11.3 38.7 %all_gather.12 = f32[1024,128]{1,0:T(8,128)S(1)} all-gather(f32[32,128]{1,0:T(8,128)S(1)} %convolution_bitcast_fusion), channel_id=1, replica_groups=mesh['plane'=16,'z_far'=4,'z_near'=4,'core'=2] {'z_far','z_near','core'}, dimensions={0}, use_global_device_ids=true | all-gather | bytes 540672 | tf_op jit(solution)/shard_map/all_gather | solution.py:59
  50.0 0.0 all-to-all-done
  50.0 0.6 fusion.3
  50.6 0.5 fusion.1
  51.1 0.0 copy-start.3
  51.2 2.1 %collective-permute-start = (f32[64,1280]{1,0:T(8,128)S(1)}, f32[64,1280]{1,0:T(8,128)S(1)}, u32[]{:S(2)}, u32[]{:S(2)}) collective-permute-start(f32[64,1280]{1,0:T(8,128)S(1)} %fusion.1), channel_id=1, source_target_pairs={{0,1},{1,0},{2,3},{3,2},{4,5},{5,4},{6,7},{7,6},{8,9},{9,8},{10,11... | collective-permute-start | bytes 983048 | tf_op jit(solution)/shard_map/ppermute | solution.py:30
  53.2 1.4 %collective-permute-done = f32[64,1280]{1,0:T(8,128)S(1)} collective-permute-done((f32[64,1280]{1,0:T(8,128)S(1)}, f32[64,1280]{1,0:T(8,128)S(1)}, u32[]{:S(2)}, u32[]{:S(2)}) %collective-permute-start) | collective-permute-done | bytes 327712 | tf_op jit(solution)/shard_map/ppermute | solution.py:30
  54.7 0.5 convolution_add_fusion
  55.2 0.0 copy-start.1
  55.2 12.1 %all_to_all.15 = f32[4,16,1280]{2,1,0:T(8,128)S(1)} all-to-all(f32[4,16,1280]{2,1,0:T(8,128)S(1)} %bitcast.18), channel_id=1, replica_groups={{0,2,6,4},{1,3,7,5},{8,10,14,12},{9,11,15,13},{16,18,22,20},{17,19,23,2..., dimensions={0} | all-to-all | bytes 655360 | tf_op jit(solution)/shard_map/all_to_all | solution.py:34
  67.3 0.0 copy-start.2
  67.3 17.8 %all-gather = f32[64,1280]{1,0:T(8,128)S(1)} all-gather(f32[16,1280]{1,0:T(8,128)S(1)} %reduce_sum.27), channel_id=2, replica_groups=mesh['plane'=16,'z_far'=4,'z_near'=4,'core'=2] {'z_far'}, dimensions={0}, use_global_device_ids=true | all-gather | bytes 409600 | tf_op jit(solution)/shard_map/all_gather | solution.py:74
  85.1 17.4 %all_gather.15 = f32[128,1280]{1,0:T(8,128)S(1)} all-gather(f32[16,1280]{1,0:T(8,128)S(1)} %reduce_sum.28), channel_id=1, replica_groups={{0,1,2,3,6,7,4,5},{8,9,10,11,14,15,12,13},{16,17,18,19,22,23,20,21},{24..., dimensions={0}, use_global_device_ids=true | all-gather | bytes 737280 | tf_op jit(solution)/shard_map/all_gather | solution.py:75
  102.5 0.0 copy-done.3
  102.5 0.7 convolution_subtract_fusion
  103.2 0.3 fusion.8
  103.5 14.0 %all_to_all.16 = f32[16,16,256]{2,1,0:T(8,128)S(1)} all-to-all(f32[16,16,256]{2,1,0:T(8,128)S(1)} %bitcast.21), channel_id=1, replica_groups={{64,384,0,448,32,160,96,224,320,128,256,192,288,416,352,480},{65,385,1,..., dimensions={0} | all-to-all | bytes 524288 | tf_op jit(solution)/shard_map/all_to_all | solution.py:34
  117.6 0.0 copy-done.2
  117.6 0.6 multiply_subtract_fusion
  (8 shorter events, 0.1 us)
Async XLA Ops:
  0.0 11.1 %copy-start = (f32[256,32]{0,1:T(8,128)S(1)}, f32[256,32]{0,1:T(8,128)}, u32[]{:S(2)}) copy-start(f32[256,32]{0,1:T(8,128)} %param.7) | copy-start | bytes 98308
  2.5 8.6 %copy-start.4 = (s32[128]{0:T(128)S(1)}, s32[128]{0:T(128)}, u32[]{:S(2)}) copy-start(s32[128]{0:T(128)} %param.8) | copy-start | bytes 1540
  2.6 47.5 %all-to-all-start = ((f32[16,16,2304]{2,1,0:T(8,128)}), f32[16,16,2304]{2,1,0:T(8,128)S(1)}, u32[]{:S(2)}, u32[]{:S(2)}) async-start(f32[16,16,2304]{2,1,0:T(8,128)} %broadcast_in_dim.2), calls=%async_computation | async-start | bytes 4718592 | tf_op jit(solution)/shard_map/all_to_all | solution.py:34
  51.1 51.4 %copy-start.3 = (f32[1024]{0:T(1024)S(1)}, f32[1024]{0:T(1024)}, u32[]{:S(2)}) copy-start(f32[1024]{0:T(1024)} %param.13) | copy-start | bytes 12292
  51.2 3.5 %collective-permute-start = (f32[64,1280]{1,0:T(8,128)S(1)}, f32[64,1280]{1,0:T(8,128)S(1)}, u32[]{:S(2)}, u32[]{:S(2)}) collective-permute-start(f32[64,1280]{1,0:T(8,128)S(1)} %fusion.1), channel_id=1, source_target_pairs={{0,1},{1,0},{2,3},{3,2},{4,5},{5,4},{6,7},{7,6},{8,9},{9,8},{10,11... | collective-permute-start | bytes 983048 | tf_op jit(solution)/shard_map/ppermute | solution.py:30
  55.2 48.0 %copy-start.1 = (f32[128,256]{1,0:T(8,128)S(1)}, f32[128,256]{1,0:T(8,128)}, u32[]{:S(2)}) copy-start(f32[128,256]{1,0:T(8,128)} %param.9) | copy-start | bytes 393220
  67.3 50.3 %copy-start.2 = (f32[16,256]{1,0:T(8,128)S(1)}, f32[16,256]{1,0:T(8,128)}, u32[]{:S(2)}) copy-start(f32[16,256]{1,0:T(8,128)} %param.11) | copy-start | bytes 49156

commit v7 on v6

--- a/solution.py
+++ b/solution.py
@@ -65,11 +65,13 @@
     tall = rows // (n_near * n_core)
     by_core = kernel.reshape(n_near, n_core, tall, -1)
 
-    def term_sums(of_core):
+    def term_sums(by_core, of_core):
         taken = lax.dynamic_index_in_dim(by_core, of_core, 1, keepdims=False)
         return product(taken.reshape(rows // n_core, -1), terms, 1, 0)
 
-    part = swapped(term_sums(1 - core)) + term_sums(core)
+    give, kept_rows = lax.optimization_barrier((term_sums(by_core, 1 - core), by_core))
+    come, keep = lax.optimization_barrier((swapped(give), term_sums(kept_rows, core)))
+    part = come + keep
     near_sum = exchanged(part.reshape(n_near, tall, -1), NEAR, NEAR_ORDER).sum(axis=0)
     own_sum = lax.all_gather(near_sum, FAR, axis=0).sum(axis=0)
     whole = lax.all_gather(

time: 119 us -> 118 us (level)
  transfers between devices with their start and end apart: 2 -> 2, of which waited for: 1 -> 1; matrix products, arithmetic and copies ran while one was open for 0% -> 1% of each run, Pallas kernels for 0% -> 0%
where the time goes in v7:
time: 118 us
  blocking collectives  100 us (85%)
  starting transfers between devices  10.6 us (9%)
  matrix products  2.72 us (2%)
  local copies, waits for them, and re-layouts  1.7 us (1%)
  other arithmetic  1.61 us (1%)
    all_gather x1, blocking collectives, on_device(): batch_t = lax.all_gather(picked, CENTRE, axis=0, tiled=True)  38.7 us
    all_to_all x2, blocking collectives, exchanged(): lax.all_to_all(blocks, axis, split_axis=0, concat_axis=0, axis_index_grou...  26.7 us
    all_gather x1, blocking collectives, on_device(): own_sum = lax.all_gather(near_sum, FAR, axis=0).sum(axis=0)  17.7 us
    all_gather x1, blocking collectives, on_device(): lax.all_gather(own_sum, NEAR_CORE, axis_index_groups=NEAR_CORE_ORDER, axi...  17 us
    all_to_all x1, starting transfers between devices, exchanged(): lax.all_to_all(blocks, axis, split_axis=0, concat_axis=0, axis_index_grou...  8.54 us
    dot_general x6, matrix products, product(): lax.dot_general(left, right, (((left_dim,), (right_dim,)), ((), ())), pre...  2.72 us
  transfers between devices with their start and end apart: 2, of which 1 were waited for; matrix products, arithmetic and copies ran while one was open for 1% of the time, Pallas kernels for 0%

profile of v7, /device:TPU:1, one launch (start us, length us, event | category | flops | bytes accessed | tf_op | source)
XLA Modules:
  0.0 117.7 jit_solution(12965106669751825569)
XLA Ops:
  0.0 0.0 copy-start
  0.0 0.9 pad_maximum_fusion
  0.9 1.6 %broadcast_in_dim.2 = f32[16,16,2304]{2,1,0:T(8,128)} broadcast(f32[16,2304]{1,0:T(8,128)S(1)} %pad_maximum_fusion), dimensions={1,2} | broadcast | bytes 2506752 | tf_op jit(solution)/shard_map/broadcast_in_dim | solution.py:40
  2.6 8.5 %all-to-all-start = ((f32[16,16,2304]{2,1,0:T(8,128)}), f32[16,16,2304]{2,1,0:T(8,128)S(1)}, u32[]{:S(2)}, u32[]{:S(2)}) async-start(f32[16,16,2304]{2,1,0:T(8,128)} %broadcast_in_dim.2), calls=%async_computation | async-start | bytes 4718592 | tf_op jit(solution)/shard_map/all_to_all | solution.py:34
  11.1 0.0 copy-done
  11.1 0.0 copy-done.4
  11.1 0.2 convolution_bitcast_fusion
  11.3 38.7 %all_gather.12 = f32[1024,128]{1,0:T(8,128)S(1)} all-gather(f32[32,128]{1,0:T(8,128)S(1)} %convolution_bitcast_fusion), channel_id=1, replica_groups=mesh['plane'=16,'z_far'=4,'z_near'=4,'core'=2] {'z_far','z_near','core'}, dimensions={0}, use_global_device_ids=true | all-gather | bytes 540672 | tf_op jit(solution)/shard_map/all_gather | solution.py:59
  50.0 0.0 all-to-all-done
  50.0 0.6 fusion.4
  50.6 0.5 fusion.2
  51.1 2.1 %collective-permute-start = (f32[64,1280]{1,0:T(8,128)S(1)}, f32[64,1280]{1,0:T(8,128)S(1)}, u32[]{:S(2)}, u32[]{:S(2)}) collective-permute-start(f32[64,1280]{1,0:T(8,128)S(1)} %fusion.2), channel_id=1, source_target_pairs={{0,1},{1,0},{2,3},{3,2},{4,5},{5,4},{6,7},{7,6},{8,9},{9,8},{10,11... | collective-permute-start | bytes 983048 | tf_op jit(solution)/shard_map/ppermute | solution.py:30
  53.2 0.0 copy-start.3
  53.3 0.5 fusion
  53.8 0.9 collective-permute-done
  54.7 0.0 copy-start.1
  54.7 12.1 %all_to_all.15 = f32[4,16,1280]{2,1,0:T(8,128)S(1)} all-to-all(f32[4,16,1280]{2,1,0:T(8,128)S(1)} %bitcast.19), channel_id=1, replica_groups={{0,2,6,4},{1,3,7,5},{8,10,14,12},{9,11,15,13},{16,18,22,20},{17,19,23,2..., dimensions={0} | all-to-all | bytes 655360 | tf_op jit(solution)/shard_map/all_to_all | solution.py:34
  66.8 0.0 copy-start.2
  66.8 17.7 %all-gather = f32[64,1280]{1,0:T(8,128)S(1)} all-gather(f32[16,1280]{1,0:T(8,128)S(1)} %reduce_sum.27), channel_id=2, replica_groups=mesh['plane'=16,'z_far'=4,'z_near'=4,'core'=2] {'z_far'}, dimensions={0}, use_global_device_ids=true | all-gather | bytes 409600 | tf_op jit(solution)/shard_map/all_gather | solution.py:76
  84.5 17.0 %all_gather.15 = f32[128,1280]{1,0:T(8,128)S(1)} all-gather(f32[16,1280]{1,0:T(8,128)S(1)} %reduce_sum.28), channel_id=1, replica_groups={{0,1,2,3,6,7,4,5},{8,9,10,11,14,15,12,13},{16,17,18,19,22,23,20,21},{24..., dimensions={0}, use_global_device_ids=true | all-gather | bytes 737280 | tf_op jit(solution)/shard_map/all_gather | solution.py:77
  101.5 0.7 convolution_subtract_fusion
  102.1 0.3 fusion.9
  102.4 14.6 %all_to_all.16 = f32[16,16,256]{2,1,0:T(8,128)S(1)} all-to-all(f32[16,16,256]{2,1,0:T(8,128)S(1)} %bitcast.22), channel_id=1, replica_groups={{64,384,0,448,32,160,96,224,320,128,256,192,288,416,352,480},{65,385,1,..., dimensions={0} | all-to-all | bytes 524288 | tf_op jit(solution)/shard_map/all_to_all | solution.py:34
  117.1 0.6 multiply_subtract_fusion
  (10 shorter events, 0.1 us)
Async XLA Ops:
  0.0 11.1 %copy-start = (f32[256,32]{0,1:T(8,128)S(1)}, f32[256,32]{0,1:T(8,128)}, u32[]{:S(2)}) copy-start(f32[256,32]{0,1:T(8,128)} %param.7) | copy-start | bytes 98308
  2.6 8.6 %copy-start.4 = (s32[128]{0:T(128)S(1)}, s32[128]{0:T(128)}, u32[]{:S(2)}) copy-start(s32[128]{0:T(128)} %param.8) | copy-start | bytes 1540
  2.6 47.5 %all-to-all-start = ((f32[16,16,2304]{2,1,0:T(8,128)}), f32[16,16,2304]{2,1,0:T(8,128)S(1)}, u32[]{:S(2)}, u32[]{:S(2)}) async-start(f32[16,16,2304]{2,1,0:T(8,128)} %broadcast_in_dim.2), calls=%async_computation | async-start | bytes 4718592 | tf_op jit(solution)/shard_map/all_to_all | solution.py:34
  51.1 3.5 %collective-permute-start = (f32[64,1280]{1,0:T(8,128)S(1)}, f32[64,1280]{1,0:T(8,128)S(1)}, u32[]{:S(2)}, u32[]{:S(2)}) collective-permute-start(f32[64,1280]{1,0:T(8,128)S(1)} %fusion.2), channel_id=1, source_target_pairs={{0,1},{1,0},{2,3},{3,2},{4,5},{5,4},{6,7},{7,6},{8,9},{9,8},{10,11... | collective-permute-start | bytes 983048 | tf_op jit(solution)/shard_map/ppermute | solution.py:30
  53.2 48.2 %copy-start.3 = (f32[1024]{0:T(1024)S(1)}, f32[1024]{0:T(1024)}, u32[]{:S(2)}) copy-start(f32[1024]{0:T(1024)} %param.13) | copy-start | bytes 12292
  54.7 47.4 %copy-start.1 = (f32[128,256]{1,0:T(8,128)S(1)}, f32[128,256]{1,0:T(8,128)}, u32[]{:S(2)}) copy-start(f32[128,256]{1,0:T(8,128)} %param.9) | copy-start | bytes 393220
  66.8 50.3 %copy-start.2 = (f32[16,256]{1,0:T(8,128)S(1)}, f32[16,256]{1,0:T(8,128)}, u32[]{:S(2)}) copy-start(f32[16,256]{1,0:T(8,128)} %param.11) | copy-start | bytes 49156
